TPU v7x, 256 devices: a whole 4x4x8 slice. The times are simulated.
256 devices in a mesh: dp: 16 (over z, core), slab: 4 (over x), fsdp: 4 (over y).
Axes of the slice: x: 4, y: 4, z: 8, core: 2. Of those that a mesh axis runs over, the one named last changes fastest.
Arguments:
- pixels: bfloat16 [16, 4, 16, 3, 224, 224], P('dp', 'fsdp', 'slab'), may hold values from -6 to 6
- grad_norm: bfloat16 [4, 4, 8192, 1280], P('slab', 'fsdp', 'dp'), may hold values from -0.015625 to 0.015625
- grad_resid: bfloat16 [4, 4, 8192, 1280], P('slab', 'fsdp', 'dp'), may hold values from -0.015625 to 0.015625
- embed_weight: bfloat16 [1280, 1176], P('fsdp'), may hold values from -0.1875 to 0.1875
- norm_gain: float32 [1280], replicated, may hold values from 0.1 to 1.9
- send_slot: int32 [4, 4, 8192], P('slab', 'fsdp', 'dp'), may hold values from 0 to 1023, as said below
- recv_slot: int32 [4, 4, 8192], P('slab', 'fsdp', 'dp'), may hold values from 0 to 1023, as said below
Outputs:
- embed_grad: float32 [1280, 1176], P('fsdp')
- norm_grad: float32 [2, 1280], P(None, 'fsdp')
Inputs may be any that keep to these rules, and one draw needn't show every extreme that they name: `send_slot`: within each slab and fsdp index, the rows of the dp group are a one-to-one map onto the tokens of the group's slab owners: each device sends all its 512 rows and its tokens receive exactly 512; the ranks of the rows from one device to one device run from 0 up without gaps; at most 64 rows go from one device to one device, and that many do in every draw. `recv_slot`: the inverse of send_slot: the values of one device are distinct and name each row that is sent to it exactly once.
All inputs are finite; a program needn't handle non-finite values.
Results may differ from a plain program's by a relative error of at most 0.0029.
Values may be sent and summed in bfloat16 or wider, within the bound.
No kernel may reach another device: no remote copies, remote signals or barrier semaphores. Data moves between devices by JAX's collectives and lax.ppermute only.
A program may use at most 128 MiB of HBM per device.

v0:
```python
import jax
import jax.numpy as jnp
import numpy as np
from jax import lax
from jax.experimental import pallas as pl
from jax.experimental.pallas import tpu as pltpu
from jax.sharding import Mesh
from jax.sharding import PartitionSpec as P

GH = 16
GW = 16
PS = 14
COLOURS = 3
SIDE = 224
ROWS = 512
CAP = 64
PEERS = 16
D = 1280
KIN = 1176
GROUPS = 9
PARTS = COLOURS * PS
FRAME = PARTS * PS
HELD = 296
HALF = 640
TILES = HALF // 128
OWNED = D // 4
LINE = OWNED * TILES
QUARTER = LINE // 4
STEP = 80
PIECE = 56
BLOCK = 128
SUMS = 96
ALL = pl.BlockSpec(memory_space=pltpu.VMEM)
FAR = pl.BlockSpec(memory_space=pltpu.HBM)
SCALAR = pl.BlockSpec(memory_space=pltpu.SMEM)
PARAMS = pltpu.CompilerParams(vmem_limit_bytes=24 * 1024 * 1024)
NORM = pltpu.CompilerParams(vmem_limit_bytes=49 * 1024 * 1024)
WIDE = pltpu.CompilerParams(vmem_limit_bytes=60 * 1024 * 1024)
LANES = (((1,), (1,)), ((), ()))
SUBLANES = (((0,), (0,)), ((), ()))


def one_hot(match):
    return match.astype(jnp.float32).astype(jnp.bfloat16)


def iota(shape, dim):
    return lax.broadcasted_iota(jnp.int32, shape, dim)


def dot(a, b, dims=(((1,), (0,)), ((), ()))):
    return lax.dot_general(a, b, dims, preferred_element_type=jnp.float32)


def column_places():
    place = np.zeros((1, KIN), np.int32)
    for c in range(COLOURS):
        for t in range(2):
            part = c * PS * PS + np.arange(PS * PS)
            at = (c * 2 + t) * PS * PS
            place[0, at : at + PS * PS] = (1 - t) * HALF + part
    return place


def patch_kernel(valid_ref, slot_ref, fa_ref, fb_ref, out_ref, spread_ref, rows_ref):
    src = iota((SIDE, 256), 0)
    place = jnp.where(src >= GROUPS * PS, src + 2, src)
    spread = one_hot(iota((SIDE, 256), 1) == place)
    for k, ref in enumerate((fa_ref, fb_ref)):
        for c in range(COLOURS):
            wide = dot(ref[0, 0, 0, c], spread)
            for h in range(2):
                spread_ref[k, c, h] = wide[:, h * 128 : (h + 1) * 128]

    @pl.when(valid_ref[0] == 0)
    def _():
        spread_ref[0] = jnp.zeros_like(spread_ref[0])

    lane = iota((GH, 128), 1)
    for k in range(2):
        for x in range(GW):
            here = slice((k * GW + x) * GH, (k * GW + x + 1) * GH)
            acc = None
            for n in range(PARTS):
                c, p = divmod(n, PS)
                piece = spread_ref[k, c, x // GROUPS, pl.ds(p, GH, stride=PS), :]
                shift = PS * (n - x % GROUPS) % 128
                if shift:
                    piece = pltpu.roll(piece, shift, 1)
                tile, at = divmod(PS * n, 128)
                acc = piece if acc is None else jnp.where(lane >= at, piece, acc)
                if n == PARTS - 1:
                    acc = jnp.where(lane < at + PS, acc, 0.0)
                if at + PS >= 128 or n == PARTS - 1:
                    rows_ref[here, tile * 128 : (tile + 1) * 128] = acc.astype(jnp.bfloat16)
                    acc = piece
    slots = slot_ref[...]
    kind = iota((16, ROWS), 0)
    digits = jnp.where(kind == 0, slots >> 6, jnp.where(kind == 1, slots & 63, 0))
    dst = iota((ROWS, ROWS), 0)
    order = one_hot(iota((ROWS, ROWS), 1) == (dst & 256) + ((dst & 15) << 4) + ((dst >> 4) & 15))
    digits = dot(order, digits.astype(jnp.float32).astype(jnp.bfloat16), LANES)
    slots = (digits[:, 0:1] * 64.0 + digits[:, 1:2]).astype(jnp.int32)
    side = iota((HELD, 128), 1) < CAP
    for i in range(PEERS // 4):
        pick = one_hot(iota((ROWS, 256), 1) + i * 256 == slots)
        both = dot(rows_ref[...], pick, SUBLANES)
        for j in range(2):
            lo = both[0:HELD, j * 128 : (j + 1) * 128]
            hi = both[HELD : 2 * HELD, j * 128 : (j + 1) * 128]
            peer = i * 4 + j * 2
            out_ref[peer] = jnp.where(side, lo, pltpu.roll(hi, CAP, 1)).astype(jnp.bfloat16)
            out_ref[peer + 1] = jnp.where(side, pltpu.roll(lo, CAP, 1), hi).astype(jnp.bfloat16)


def packed_rows(valid, slots, first, second, first_at, second_at):
    block = (1, 1, 1, COLOURS, SIDE, SIDE)
    shape = (PEERS, HELD, 128)
    return pl.pallas_call(
        patch_kernel,
        out_shape=jax.ShapeDtypeStruct(shape, jnp.bfloat16),
        grid=(1,),
        in_specs=[
            SCALAR,
            pl.BlockSpec((1, ROWS), lambda i: (0, 0)),
            pl.BlockSpec(block, lambda i: (0, 0, first_at, 0, 0, 0)),
            pl.BlockSpec(block, lambda i: (0, 0, second_at, 0, 0, 0)),
        ],
        out_specs=pl.BlockSpec(shape, lambda i: (0, 0, 0)),
        scratch_shapes=[
            pltpu.VMEM((2, COLOURS, 2, SIDE, 128), jnp.float32),
            pltpu.VMEM((ROWS, HALF), jnp.bfloat16),
        ],
        compiler_params=WIDE,
        name="patch_rows",
    )(valid, slots, first, second)


def weight_kernel(place_ref, column_ref, own_ref, *refs):
    *parts, out_ref, held_ref = refs
    core, y = place_ref[0], place_ref[2]
    part = OWNED // 2
    held_ref[pl.ds(pl.multiple_of(y * OWNED, 16), OWNED), :] = own_ref[...]
    for n, ref in enumerate(parts):
        side, by = divmod(n, 3)
        row = ((y - by - 1) & 3) * OWNED + (core if side == 0 else 1 - core) * part
        held_ref[pl.ds(pl.multiple_of(row, 16), part), :] = ref[...]
    for i in range(2):
        pick = one_hot(iota((HALF, KIN), 0) + i * HALF == column_ref[...])
        out_ref[:, i * HALF : (i + 1) * HALF] = dot(held_ref[...], pick, LANES).astype(jnp.bfloat16)


def padded_weight(place, own, parts):
    return pl.pallas_call(
        weight_kernel,
        out_shape=jax.ShapeDtypeStruct((D, 2 * HALF), jnp.bfloat16),
        in_specs=[SCALAR] + [ALL] * 8,
        out_specs=ALL,
        scratch_shapes=[pltpu.VMEM((D, KIN), jnp.bfloat16)],
        compiler_params=WIDE,
        name="weight_columns",
    )(place, jnp.asarray(column_places()), own, *parts)


def taken_rows(slot_ref, arr_ref, cols_ref):
    side = iota((HELD, 128), 1) < CAP
    for j in range(PEERS // 2):
        even = arr_ref[2 * j].astype(jnp.float32)
        odd = arr_ref[2 * j + 1].astype(jnp.float32)
        low = jnp.where(side, even, pltpu.roll(odd, CAP, 1))
        high = jnp.where(side, pltpu.roll(even, CAP, 1), odd)
        both = jnp.concatenate([low, high], axis=0).astype(jnp.bfloat16)
        cols_ref[: 2 * HELD, j * 128 : (j + 1) * 128] = both
    cols_ref[2 * HELD :, :] = jnp.zeros((HALF - 2 * HELD, PEERS * CAP), jnp.bfloat16)
    pick = one_hot(iota((ROWS, PEERS * CAP), 1) == slot_ref[...])
    return dot(pick, cols_ref[...], LANES).astype(jnp.bfloat16)


def first_kernel(slot_ref, arr_ref, w_ref, part_ref, cols_ref, rows_ref):
    rows_ref[...] = taken_rows(slot_ref, arr_ref, cols_ref)

    def block(i, carry):
        here = pl.ds(pl.multiple_of(i * 128, 128), 128)
        part_ref[here, :D] = dot(rows_ref[here, :], w_ref[:, :HALF], LANES)
        part_ref[here, D:] = rows_ref[here, :].astype(jnp.float32)
        return carry

    lax.fori_loop(0, ROWS // 128, block, 0)


def first_half(slots, arrived, weight):
    return pl.pallas_call(
        first_kernel,
        out_shape=jax.ShapeDtypeStruct((ROWS, D + HALF), jnp.float32),
        in_specs=[ALL] * 3,
        out_specs=ALL,
        scratch_shapes=[
            pltpu.VMEM((HALF, PEERS * CAP), jnp.bfloat16),
            pltpu.VMEM((ROWS, HALF), jnp.bfloat16),
        ],
        compiler_params=WIDE,
        name="first_half",
    )(slots, arrived, weight)


def backward_kernel(core_ref, slot_ref, arr_ref, part_far, w_far, g_far, r_far, gain_ref, grad_ref, mine_ref, send_ref, sums_ref, cols_ref, rows1_ref, part_ref, w_ref, g_ref, r_ref, sems):
    reads = [
        pltpu.make_async_copy(w_far.at[:, HALF:], w_ref, sems.at[0]),
        pltpu.make_async_copy(part_far, part_ref, sems.at[1]),
        pltpu.make_async_copy(g_far.at[0, 0], g_ref, sems.at[2]),
        pltpu.make_async_copy(r_far.at[0, 0], r_ref, sems.at[3]),
    ]
    for read in reads:
        read.start()
    rows1_ref[...] = taken_rows(slot_ref, arr_ref, cols_ref)
    for read in reads:
        read.wait()

    @pl.when(core_ref[0] == 0)
    def _():
        mine_ref[...] = part_ref[:, D:].astype(jnp.bfloat16)
        send_ref[...] = rows1_ref[...]

    @pl.when(core_ref[0] != 0)
    def _():
        mine_ref[...] = rows1_ref[...]
        send_ref[...] = part_ref[:, D:].astype(jnp.bfloat16)

    sums_ref[...] = jnp.zeros_like(sums_ref)

    def block(i, carry):
        here = pl.ds(pl.multiple_of(i * BLOCK, BLOCK), BLOCK)
        embedded = part_ref[here, :D] + dot(rows1_ref[here, :], w_ref[...], LANES)
        deviation = embedded - jnp.mean(embedded, axis=-1, keepdims=True)
        variance = jnp.mean(deviation * deviation, axis=-1, keepdims=True)
        inverse_std = lax.rsqrt(variance + 1e-06)
        normalized = deviation * inverse_std
        upstream_norm = g_ref[here, :].astype(jnp.float32)
        upstream = upstream_norm * gain_ref[...]
        inner = jnp.mean(upstream * normalized, axis=-1, keepdims=True)
        level = jnp.mean(upstream, axis=-1, keepdims=True)
        input_grad = r_ref[here, :].astype(jnp.float32) + inverse_std * (
            upstream - level - normalized * inner
        )
        grad_ref[here, :] = input_grad.astype(jnp.bfloat16)
        sums_ref[0:8, :] += jnp.sum((upstream_norm * normalized).reshape(BLOCK // 8, 8, D), axis=0)
        sums_ref[8:16, :] += jnp.sum(upstream_norm.reshape(BLOCK // 8, 8, D), axis=0)
        return carry

    lax.fori_loop(0, ROWS // BLOCK, block, 0)


def norm_backward(core, slots, arrived, part, weight, grad_norm, grad_resid, gain):
    half = jax.ShapeDtypeStruct((ROWS, HALF), jnp.bfloat16)
    return pl.pallas_call(
        backward_kernel,
        out_shape=(
            jax.ShapeDtypeStruct((ROWS, D), jnp.bfloat16),
            half,
            half,
            jax.ShapeDtypeStruct((16, D), jnp.float32),
        ),
        in_specs=[SCALAR, ALL, ALL, FAR, FAR, FAR, FAR, ALL],
        out_specs=(ALL,) * 4,
        scratch_shapes=[
            pltpu.VMEM((HALF, PEERS * CAP), jnp.bfloat16),
            pltpu.VMEM((ROWS, HALF), jnp.bfloat16),
            pltpu.VMEM((ROWS, D + HALF), jnp.float32),
            pltpu.VMEM((D, HALF), jnp.bfloat16),
            pltpu.VMEM((ROWS, D), jnp.bfloat16),
            pltpu.VMEM((ROWS, D), jnp.bfloat16),
            pltpu.SemaphoreType.DMA((4,)),
        ],
        compiler_params=NORM,
        name="norm_backward",
    )(core, slots, arrived, part, weight, grad_norm, grad_resid, gain)


def product_kernel(core_ref, grad0_ref, grad1_ref, rows0_ref, rows1_ref, sums_ref, own_ref, out1_ref, out2_ref, out3_ref, terms_ref, order_ref):
    core, place = core_ref[0], core_ref[1]
    kind = iota((128, HALF), 0)
    for i in range(D // HALF):
        here = slice(i * HALF, (i + 1) * HALF)
        terms_ref[...] = dot(grad0_ref[:, here], rows0_ref[...], SUBLANES) + dot(
            grad1_ref[:, here], rows1_ref[...], SUBLANES
        )
        gain_sum = jnp.sum(sums_ref[0:8, here], axis=0, keepdims=True)
        bias_sum = jnp.sum(sums_ref[8:16, here], axis=0, keepdims=True)
        sums = jnp.where(kind == SUMS, gain_sum, jnp.where(kind == SUMS + 1, bias_sum, 0.0))
        terms_ref[:, HALF - 128 :] += sums.T
        for n in range(HALF // STEP):
            y, r = divmod(i * (HALF // STEP) + n, OWNED // STEP)
            for t in range(TILES):
                o = t * (OWNED // STEP) + r
                block = terms_ref[n * STEP : (n + 1) * STEP, t * 128 : (t + 1) * 128]
                to = jnp.where(core == 0, y, o // 5)
                at = jnp.where(core == 0, o * STEP, y * QUARTER + o % 5 * STEP)
                at = pl.ds(pl.multiple_of(at, 16), STEP)
                order_ref[(to - place) & 3, at, :] = block
    own_ref[...] = order_ref[0]
    for by, ref in enumerate((out1_ref, out2_ref, out3_ref)):
        ref[...] = order_ref[by + 1].astype(jnp.bfloat16)


def products(core, grad0, grad1, rows0, rows1, sums):
    sent = jax.ShapeDtypeStruct((LINE, 128), jnp.bfloat16)
    return pl.pallas_call(
        product_kernel,
        out_shape=(jax.ShapeDtypeStruct((LINE, 128), jnp.float32), sent, sent, sent),
        in_specs=[SCALAR] + [ALL] * 5,
        out_specs=(ALL,) * 4,
        scratch_shapes=[
            pltpu.VMEM((HALF, HALF), jnp.float32),
            pltpu.VMEM((4, LINE, 128), jnp.float32),
        ],
        compiler_params=PARAMS,
        name="products",
    )(core, grad0, grad1, rows0, rows1, sums)


def fold_kernel(place_ref, own_ref, in1_ref, in2_ref, in3_ref, keep_ref, out1_ref, out2_ref, out3_ref, order_ref):
    place = place_ref[3]
    for d in range(4):
        at = slice(d * QUARTER, (d + 1) * QUARTER)
        block = own_ref[at, :]
        for ref in (in1_ref, in2_ref, in3_ref):
            block += ref[at, :].astype(jnp.float32)
        order_ref[(d - place) & 3] = block
    keep_ref[...] = order_ref[0]
    for by, ref in enumerate((out1_ref, out2_ref, out3_ref)):
        ref[...] = order_ref[by + 1].astype(jnp.bfloat16)


def fold(place, own, terms):
    sent = jax.ShapeDtypeStruct((QUARTER, 128), jnp.bfloat16)
    return pl.pallas_call(
        fold_kernel,
        out_shape=(jax.ShapeDtypeStruct((QUARTER, 128), jnp.float32), sent, sent, sent),
        in_specs=[SCALAR] + [ALL] * 4,
        out_specs=(ALL,) * 4,
        scratch_shapes=[pltpu.VMEM((4, QUARTER, 128), jnp.float32)],
        compiler_params=PARAMS,
        name="fold",
    )(place, own, *terms)


def runs():
    place = column_places()[0]
    found = []
    at = 0
    while at < KIN:
        stop = at + 1
        while stop < KIN and place[stop] == place[stop - 1] + 1 and place[stop] % 128 and stop % 128:
            stop += 1
        found.append((at, int(place[at]), stop - at))
        at = stop
    return found


def finish_kernel(place_ref, *refs):
    *parts, out_ref, norm_ref, held_ref, last_ref = refs
    core, x = place_ref[0], place_ref[4]
    for n, ref in enumerate(parts):
        side, by = divmod(n, 4)
        at = pl.multiple_of(((x - by) & 3) * QUARTER, 16)
        held_ref[core if side == 0 else 1 - core, pl.ds(at, QUARTER), :] = ref[...]
    lane = iota((OWNED, 128), 1)
    for tile in range(pl.cdiv(KIN, 128)):
        acc = None
        for at, src, size in runs():
            if at // 128 != tile:
                continue
            half, column = divmod(src // 128, TILES)
            piece = held_ref[half, column * OWNED : (column + 1) * OWNED, :]
            shift = (at - src) % 128
            if shift:
                piece = pltpu.roll(piece, shift, 1)
            acc = piece if acc is None else jnp.where(lane >= at % 128, piece, acc)
        width = min(128, KIN - tile * 128)
        out_ref[:, tile * 128 : tile * 128 + width] = acc[:, :width]
    last_ref[0:OWNED, :] = held_ref[0, LINE - OWNED :, :] + held_ref[1, LINE - OWNED :, :]
    last_ref[OWNED:, :] = jnp.zeros((384 - OWNED, 128), jnp.float32)
    norm_ref[...] = last_ref[...].T[SUMS : SUMS + 2, :OWNED]


def finish(place, parts):
    return pl.pallas_call(
        finish_kernel,
        out_shape=(
            jax.ShapeDtypeStruct((OWNED, KIN), jnp.float32),
            jax.ShapeDtypeStruct((2, OWNED), jnp.float32),
        ),
        in_specs=[SCALAR] + [ALL] * 8,
        out_specs=(ALL, ALL),
        scratch_shapes=[
            pltpu.VMEM((2, LINE, 128), jnp.float32),
            pltpu.VMEM((384, 128), jnp.float32),
        ],
        compiler_params=PARAMS,
        name="column_order",
    )(place, *parts)


def plane_index(core, x, y):
    return (core * 4 + x) * 4 + y


def plane_shift(by, along_y):
    pairs = []
    for x in range(4):
        for y in range(4):
            for core in range(2):
                to = (x, (y + by) % 4) if core == along_y else ((x + by) % 4, y)
                pairs.append((plane_index(core, x, y), plane_index(core, *to)))
    return pairs


def ring(by):
    return [(i, (i + by) % 4) for i in range(4)]


def copies(array, axis, count):
    array = jnp.broadcast_to(array[None], (count,) + array.shape)
    return lax.all_to_all(array, axis, 0, 0, tiled=True)


def shards(pixels, grad_norm, grad_resid, embed_weight, norm_gain, send_slot, recv_slot):
    plane = ("core", "slab", "fsdp")
    core = lax.axis_index("core").astype(jnp.int32)
    x = lax.axis_index("slab").astype(jnp.int32)
    y = lax.axis_index("fsdp").astype(jnp.int32)
    place = jnp.stack([core, jnp.where(core == 0, y, x), y, jnp.where(core == 0, x, y), x])
    earlier = lax.ppermute(pixels[:, :, 3:4], "slab", ring(1))
    takes = recv_slot.reshape(1, ROWS)
    sends = send_slot.reshape(ROWS, 1)
    packed0 = packed_rows(jnp.ones((1,), jnp.int32), takes, pixels, pixels, 0, 2)
    packed0, shard = lax.optimization_barrier((packed0, embed_weight))
    arrived0 = lax.all_to_all(packed0, ("z", "core"), 0, 0, tiled=True)
    swap = [(0, 1), (1, 0)]
    part = lax.dynamic_slice_in_dim(shard, core * (OWNED // 2), OWNED // 2, 0)
    parts = [lax.ppermute(part, "fsdp", ring(by)) for by in (1, 2, 3)]
    earlier, *parts = lax.optimization_barrier((earlier, *parts))
    packed1 = packed_rows((x > 0).astype(jnp.int32)[None], takes, earlier, pixels, 0, 1)
    arrived1 = lax.all_to_all(packed1, ("z", "core"), 0, 0, tiled=True)
    parts += [lax.ppermute(part, "core", swap) for part in parts]
    weight = padded_weight(place, embed_weight, parts)
    part = first_half(sends, arrived0, weight)
    grads, mine, send, sums = norm_backward(
        place, sends, arrived1, part, weight, grad_norm, grad_resid, norm_gain.reshape(1, D)
    )
    theirs = lax.ppermute(send, "core", swap)
    their_grads = lax.ppermute(grads, "core", swap)
    own, *sent = products(place, grads, their_grads, mine, theirs, sums)
    terms = [lax.ppermute(sent[by - 1], plane, plane_shift(by, 0)) for by in (1, 3, 2)]
    keep, *sent = fold(place, own, terms)
    terms = [lax.ppermute(sent[by - 1], plane, plane_shift(by, 1)) for by in (1, 3, 2)]
    quarter = keep + terms[0].astype(jnp.float32) + terms[1].astype(jnp.float32) + terms[2].astype(jnp.float32)
    quarter = jnp.pad(quarter, ((0, 8 * PIECE - QUARTER), (0, 0)))
    pieces = lax.all_to_all(quarter.reshape(8, PIECE, 128), "z", 0, 0, tiled=True)
    quarter = copies(jnp.sum(pieces, axis=0), "z", 8).reshape(8 * PIECE, 128)[:QUARTER]
    mine = [quarter] + [lax.ppermute(quarter, "slab", ring(by)) for by in (1, 2, 3)]
    return finish(place, mine + [lax.ppermute(part, "core", swap) for part in mine])


def solution(mesh):
    split = Mesh(mesh.devices.reshape(8, 2, 4, 4), ("z", "core", "slab", "fsdp"))
    dp = ("z", "core")
    return jax.shard_map(
        shards,
        mesh=split,
        in_specs=(
            P(dp, "fsdp", "slab", None, None, None),
            P("slab", "fsdp", dp, None),
            P("slab", "fsdp", dp, None),
            P("fsdp", None),
            P(),
            P("slab", "fsdp", dp),
            P("slab", "fsdp", dp),
        ),
        out_specs=(P("fsdp", None), P(None, "fsdp")),
        check_vma=False,
    )
```

profile of v0, /device:TPU:1, one launch (start us, length us, event | category | flops | bytes accessed | tf_op | source)
XLA Modules:
  0.0 166.2 jit_solution(12584935202874077643)
XLA Ops:
  0.6 5.3 %patch_rows.2 = bf16[16,296,128]{2,1,0:T(8,128)(2,1)} custom-call(s32[1]{0:T(128)} %constant.22.clone.1.valid_ref, s32[1,512]{1,0:T(1,128)} %bitcast.12, bf16[1,1,4,3,224,224]{5,4,3,2,1,0:T(8,128)(2,1)} %fb_ref.3, bf16[1,1,4,3,224,224]{5,4,3,2,1,0:T(8,128)(2,1)} %fb_ref.3), custom_call_target="tpu_custom_call" | custom-call | tf_op jit(solution)/shard_map/patch_rows/pallas_call | solution.py:119
  6.0 10.1 %all-to-all-start.1 = ((bf16[16,296,128]{2,1,0:T(8,128)(2,1)}), bf16[16,296,128]{2,1,0:T(8,128)(2,1)S(1)}, u32[]{:S(2)}, u32[]{:S(2)}) async-start(bf16[16,296,128]{2,1,0:T(8,128)(2,1)} %patch_rows.2), calls=%async_computation.1 | async-start | bytes 2424832 | tf_op jit(solution)/shard_map/all_to_all | solution.py:438
  16.1 2.8 %collective-permute-start.3 = (bf16[160,1176]{1,0:T(8,128)(2,1)S(1)}, bf16[160,1176]{1,0:T(8,128)(2,1)S(1)}, u32[]{:S(2)}, u32[]{:S(2)}) collective-permute-start(bf16[160,1176]{1,0:T(8,128)(2,1)S(1)} %constant_dynamic-slice_fusion), channel_id=1, source_target_pairs={{0,3},{1,0},{2,1},{3,2},{4,7},{5,4},{6,5},{7,6},{8,11},{9,8},{10,9... | collective-permute-start | bytes 1128968 | tf_op jit(solution)/shard_map/ppermute | solution.py:441
  22.3 8.7 %collective-permute-done.fa_ref = bf16[1,1,1,3,224,224]{5,4,3,2,1,0:T(8,128)(2,1)S(1)} collective-permute-done((bf16[1,1,1,3,224,224]{5,4,3,2,1,0:T(8,128)(2,1)S(1)}, bf16[1,1,1,3,224,224]{5,4,3,2,1,0:T(8,128)(2,1)S(1)}, u32[]{:S(2)}, u32[]{:S(2)}) %collective-permute-start) | collective-permute-done | bytes 301088 | tf_op jit(solution)/shard_map/ppermute | solution.py:433
  31.0 5.5 %collective-permute-done.3.refs_2_ = bf16[160,1176]{1,0:T(8,128)(2,1)S(1)} collective-permute-done((bf16[160,1176]{1,0:T(8,128)(2,1)S(1)}, bf16[160,1176]{1,0:T(8,128)(2,1)S(1)}, u32[]{:S(2)}, u32[]{:S(2)}) %collective-permute-start.3) | collective-permute-done | bytes 376352 | tf_op jit(solution)/shard_map/ppermute | solution.py:441
  36.4 4.2 %collective-permute-done.1.refs_0_ = bf16[160,1176]{1,0:T(8,128)(2,1)S(1)} collective-permute-done((bf16[160,1176]{1,0:T(8,128)(2,1)S(1)}, bf16[160,1176]{1,0:T(8,128)(2,1)S(1)}, u32[]{:S(2)}, u32[]{:S(2)}) %collective-permute-start.1) | collective-permute-done | bytes 376352 | tf_op jit(solution)/shard_map/ppermute | solution.py:441
  40.7 5.5 %patch_rows.3 = bf16[16,296,128]{2,1,0:T(8,128)(2,1)} custom-call(s32[1]{0:T(128)} %bitcast.6.valid_ref, s32[1,512]{1,0:T(1,128)} %bitcast.13, bf16[1,1,1,3,224,224]{5,4,3,2,1,0:T(8,128)(2,1)} %copy-done.7, bf16[1,1,4,3,224,224]{5,4,3,2,1,0:T(8,128)(2,1)} %fb_ref.3), custom_call_target="tpu_custom_call" | custom-call | tf_op jit(solution)/shard_map/patch_rows/pallas_call | solution.py:119
  47.3 6.2 %all-to-all-start = ((bf16[16,296,128]{2,1,0:T(8,128)(2,1)}), bf16[16,296,128]{2,1,0:T(8,128)(2,1)S(1)}, u32[]{:S(2)}, u32[]{:S(2)}) async-start(bf16[16,296,128]{2,1,0:T(8,128)(2,1)} %patch_rows.3), calls=%async_computation | async-start | bytes 2424832 | tf_op jit(solution)/shard_map/all_to_all | solution.py:444
  56.6 9.1 %weight_columns.1.w_ref.w_far = bf16[1280,1280]{1,0:T(8,128)(2,1)} custom-call(s32[5]{0:T(128)} %stack.23.place_ref.core_ref, s32[1,1176]{1,0:T(1,128)} %constant.26.clone.column_ref, bf16[320,1176]{1,0:T(8,128)(2,1)} %own_ref.1, bf16[160,1176]{1,0:T(8,128)(2,1)} %copy-done.6, bf16[160,1176]{1,0:T(8,128)(2,1)} %copy-done.5, bf16[160,1176]{1,0:T(8,128)(2,1)} %copy-done.4, ...), custom_call_target="tpu_custom_call" | custom-call | tf_op jit(solution)/shard_map/weight_columns/pallas_call | solution.py:154
  65.7 8.0 %first_half.1.part_far = f32[512,1920]{1,0:T(8,128)} custom-call(s32[512,1]{1,0:T(8,128)} %copy.11.slot_ref, bf16[16,296,128]{2,1,0:T(8,128)(2,1)} %copy-done.2, bf16[1280,1280]{1,0:T(8,128)(2,1)} %weight_columns.1.w_ref.w_far), custom_call_target="tpu_custom_call" | custom-call | tf_op jit(solution)/shard_map/first_half/pallas_call | solution.py:192
  73.7 11.1 %all-to-all-done.arr_ref = bf16[16,296,128]{2,1,0:T(8,128)(2,1)S(1)} async-done(((bf16[16,296,128]{2,1,0:T(8,128)(2,1)}), bf16[16,296,128]{2,1,0:T(8,128)(2,1)S(1)}, u32[]{:S(2)}, u32[]{:S(2)}) %all-to-all-start) | async-done | bytes 1212448 | tf_op jit(solution)/shard_map/all_to_all | solution.py:444
  84.7 8.5 %norm_backward.1 = (bf16[512,1280]{1,0:T(8,128)(2,1)S(1)}, bf16[512,640]{1,0:T(8,128)(2,1)S(1)}, bf16[512,640]{1,0:T(8,128)(2,1)S(1)}, f32[16,1280]{1,0:T(8,128)S(1)}) custom-call(s32[5]{0:T(128)S(1)} %copy-done.1, s32[512,1]{1,0:T(8,128)S(1)} %copy-done, bf16[16,296,128]{2,1,0:T(8,128)(2,1)S(1)} %all-to-all-done.arr_ref, f32[512,1920]{1,0:T(8,128)} %first_half.1.part_far, ...), custom_call_target="tpu_custom_call" | custom-call | tf_op jit(solution)/shard_map/norm_backward/pallas_call | solution.py:255
  93.9 3.5 %collective-permute-done.8.rows1_ref = bf16[512,640]{1,0:T(8,128)(2,1)S(1)} collective-permute-done((bf16[512,640]{1,0:T(8,128)(2,1)S(1)}, bf16[512,640]{1,0:T(8,128)(2,1)S(1)}, u32[]{:S(2)}, u32[]{:S(2)}) %collective-permute-start.8) | collective-permute-done | bytes 655392 | tf_op jit(solution)/shard_map/ppermute | solution.py:451
  97.3 3.2 %products.1 = (f32[1600,128]{1,0:T(8,128)S(1)}, bf16[1600,128]{1,0:T(8,128)(2,1)S(1)}, bf16[1600,128]{1,0:T(8,128)(2,1)S(1)}, bf16[1600,128]{1,0:T(8,128)(2,1)S(1)}) custom-call(s32[5]{0:T(128)S(1)} %copy-done.1, bf16[512,1280]{1,0:T(8,128)(2,1)S(1)} %get-tuple-element.26.grad0_ref, bf16[512,1280]{1,0:T(8,128)(2,1)S(1)} %collective-permute-done.7.grad1_ref, ...), custom_call_target="tpu_custom_call" | custom-call | tf_op jit(solution)/shard_map/products/pallas_call | solution.py:307
  104.8 4.1 %collective-permute-done.9.in1_ref = bf16[1600,128]{1,0:T(8,128)(2,1)S(1)} collective-permute-done((bf16[1600,128]{1,0:T(8,128)(2,1)S(1)}, bf16[1600,128]{1,0:T(8,128)(2,1)S(1)}, u32[]{:S(2)}, u32[]{:S(2)}) %collective-permute-start.9) | collective-permute-done | bytes 409632 | tf_op jit(solution)/shard_map/ppermute | solution.py:454
  108.9 3.7 %collective-permute-done.10.in2_ref = bf16[1600,128]{1,0:T(8,128)(2,1)S(1)} collective-permute-done((bf16[1600,128]{1,0:T(8,128)(2,1)S(1)}, bf16[1600,128]{1,0:T(8,128)(2,1)S(1)}, u32[]{:S(2)}, u32[]{:S(2)}) %collective-permute-start.10) | collective-permute-done | bytes 409632 | tf_op jit(solution)/shard_map/ppermute | solution.py:454
  114.8 2.7 %collective-permute-start.13 = (bf16[400,128]{1,0:T(8,128)(2,1)S(1)}, bf16[400,128]{1,0:T(8,128)(2,1)S(1)}, u32[]{:S(2)}, u32[]{:S(2)}) collective-permute-start(bf16[400,128]{1,0:T(8,128)(2,1)S(1)} %get-tuple-element.36), channel_id=1, source_target_pairs={{0,12},{16,19},{1,13},{17,16},{2,14},{18,17},{3,15},{19,18},{4,0},... | collective-permute-start | bytes 307208 | tf_op jit(solution)/shard_map/ppermute | solution.py:456
  117.5 2.3 %collective-permute-done.12 = bf16[400,128]{1,0:T(8,128)(2,1)S(1)} collective-permute-done((bf16[400,128]{1,0:T(8,128)(2,1)S(1)}, bf16[400,128]{1,0:T(8,128)(2,1)S(1)}, u32[]{:S(2)}, u32[]{:S(2)}) %collective-permute-start.12) | collective-permute-done | bytes 102432 | tf_op jit(solution)/shard_map/ppermute | solution.py:456
  122.6 11.9 %all_to_all.20 = f32[8,56,128]{2,1,0:T(8,128)S(1)} all-to-all(f32[8,56,128]{2,1,0:T(8,128)S(1)} %bitcast.10), channel_id=1, replica_groups=mesh['z'=8,'core'=2,'slab'=4,'fsdp'=4] {'z'}, dimensions={0} | all-to-all | bytes 458752 | tf_op jit(solution)/shard_map/all_to_all | solution.py:459
  134.5 11.4 %all_to_all.21 = f32[8,56,128]{2,1,0:T(8,128)S(1)} all-to-all(f32[8,56,128]{2,1,0:T(8,128)S(1)} %broadcast_in_dim.13), channel_id=1, replica_groups=mesh['z'=8,'core'=2,'slab'=4,'fsdp'=4] {'z'}, dimensions={0} | all-to-all | bytes 458752 | tf_op jit(solution)/shard_map/all_to_all | solution.py:424
  146.0 2.9 %collective-permute-start.17 = (f32[400,128]{1,0:T(8,128)S(1)}, f32[400,128]{1,0:T(8,128)S(1)}, u32[]{:S(2)}, u32[]{:S(2)}) collective-permute-start(f32[400,128]{1,0:T(8,128)S(1)} %slice.8.refs_0_), channel_id=1, source_target_pairs={{0,12},{4,0},{8,4},{12,8},{1,13},{5,1},{9,5},{13,9},{2,14},{6,2},{... | collective-permute-start | bytes 614408 | tf_op jit(solution)/shard_map/ppermute | solution.py:461
  149.6 4.5 %collective-permute-start.18 = (f32[400,128]{1,0:T(8,128)S(1)}, f32[400,128]{1,0:T(8,128)S(1)}, u32[]{:S(2)}, u32[]{:S(2)}) collective-permute-start(f32[400,128]{1,0:T(8,128)S(1)} %slice.8.refs_0_), channel_id=1, source_target_pairs={{0,16},{16,0},{1,17},{17,1},{2,18},{18,2},{3,19},{19,3},{4,20},{20... | collective-permute-start | bytes 614408 | tf_op jit(solution)/shard_map/ppermute | solution.py:462
  154.0 4.6 %collective-permute-start.21 = (f32[400,128]{1,0:T(8,128)S(1)}, f32[400,128]{1,0:T(8,128)S(1)}, u32[]{:S(2)}, u32[]{:S(2)}) collective-permute-start(f32[400,128]{1,0:T(8,128)S(1)} %collective-permute-done.17.refs_3_), channel_id=1, source_target_pairs={{0,16},{16,0},{1,17},{17,1},{2,18},{18,2},{3,19},{19,3},{4,20},{20... | collective-permute-start | bytes 614408 | tf_op jit(solution)/shard_map/ppermute | solution.py:462
  163.5 2.7 %column_order.1 = (f32[320,1176]{1,0:T(8,128)}, f32[2,320]{1,0:T(2,128)}) custom-call(s32[5]{0:T(128)S(1)} %copy-done.1, f32[400,128]{1,0:T(8,128)S(1)} %slice.8.refs_0_, f32[400,128]{1,0:T(8,128)S(1)} %collective-permute-done.15.refs_1_, f32[400,128]{1,0:T(8,128)S(1)} %collective-permute-done.16.refs_2_, f32[400,128]{1,0:T(8,128)S(1)} %collective-permute-done.17.refs_3_, ...), custom_call_target="tpu_custom_call" | custom-call | tf_op jit(solution)/shard_map/column_order/pallas_call | solution.py:387
  (64 shorter events, 23.0 us)
Async XLA Ops:
  6.0 41.3 %all-to-all-start.1 = ((bf16[16,296,128]{2,1,0:T(8,128)(2,1)}), bf16[16,296,128]{2,1,0:T(8,128)(2,1)S(1)}, u32[]{:S(2)}, u32[]{:S(2)}) async-start(bf16[16,296,128]{2,1,0:T(8,128)(2,1)} %patch_rows.2), calls=%async_computation.1 | async-start | bytes 2424832 | tf_op jit(solution)/shard_map/all_to_all | solution.py:438
  16.1 20.3 %collective-permute-start.3 = (bf16[160,1176]{1,0:T(8,128)(2,1)S(1)}, bf16[160,1176]{1,0:T(8,128)(2,1)S(1)}, u32[]{:S(2)}, u32[]{:S(2)}) collective-permute-start(bf16[160,1176]{1,0:T(8,128)(2,1)S(1)} %constant_dynamic-slice_fusion), channel_id=1, source_target_pairs={{0,3},{1,0},{2,1},{3,2},{4,7},{5,4},{6,5},{7,6},{8,11},{9,8},{10,9... | collective-permute-start | bytes 1128968 | tf_op jit(solution)/shard_map/ppermute | solution.py:441
  19.0 17.4 %collective-permute-start.2 = (bf16[160,1176]{1,0:T(8,128)(2,1)S(1)}, bf16[160,1176]{1,0:T(8,128)(2,1)S(1)}, u32[]{:S(2)}, u32[]{:S(2)}) collective-permute-start(bf16[160,1176]{1,0:T(8,128)(2,1)S(1)} %constant_dynamic-slice_fusion), channel_id=1, source_target_pairs={{0,2},{1,3},{2,0},{3,1},{4,6},{5,7},{6,4},{7,5},{8,10},{9,11},{10,... | collective-permute-start | bytes 1128968 | tf_op jit(solution)/shard_map/ppermute | solution.py:441
  19.3 21.3 %collective-permute-start.1 = (bf16[160,1176]{1,0:T(8,128)(2,1)S(1)}, bf16[160,1176]{1,0:T(8,128)(2,1)S(1)}, u32[]{:S(2)}, u32[]{:S(2)}) collective-permute-start(bf16[160,1176]{1,0:T(8,128)(2,1)S(1)} %constant_dynamic-slice_fusion), channel_id=1, source_target_pairs={{0,1},{1,2},{2,3},{3,0},{4,5},{5,6},{6,7},{7,4},{8,9},{9,10},{10,1... | collective-permute-start | bytes 1128968 | tf_op jit(solution)/shard_map/ppermute | solution.py:441
  21.0 9.9 %collective-permute-start = (bf16[1,1,1,3,224,224]{5,4,3,2,1,0:T(8,128)(2,1)S(1)}, bf16[1,1,1,3,224,224]{5,4,3,2,1,0:T(8,128)(2,1)S(1)}, u32[]{:S(2)}, u32[]{:S(2)}) collective-permute-start(bf16[1,1,1,3,224,224]{5,4,3,2,1,0:T(8,128)(2,1)S(1)} %slice.6), channel_id=1, source_target_pairs={{0,4},{4,8},{8,12},{12,0},{1,5},{5,9},{9,13},{13,1},{2,6},{6,10},{... | collective-permute-start | bytes 903176 | tf_op jit(solution)/shard_map/ppermute | solution.py:433
  47.3 37.4 %all-to-all-start = ((bf16[16,296,128]{2,1,0:T(8,128)(2,1)}), bf16[16,296,128]{2,1,0:T(8,128)(2,1)S(1)}, u32[]{:S(2)}, u32[]{:S(2)}) async-start(bf16[16,296,128]{2,1,0:T(8,128)(2,1)} %patch_rows.3), calls=%async_computation | async-start | bytes 2424832 | tf_op jit(solution)/shard_map/all_to_all | solution.py:444
  53.5 2.3 %collective-permute-start.4 = (bf16[160,1176]{1,0:T(8,128)(2,1)}, bf16[160,1176]{1,0:T(8,128)(2,1)}, u32[]{:S(2)}, u32[]{:S(2)}) collective-permute-start(bf16[160,1176]{1,0:T(8,128)(2,1)} %copy-done.6), channel_id=1, source_target_pairs={{0,16},{16,0},{1,17},{17,1},{2,18},{18,2},{3,19},{19,3},{4,20},{20... | collective-permute-start | bytes 1128968 | tf_op jit(solution)/shard_map/ppermute | solution.py:445
  53.7 2.3 %collective-permute-start.5 = (bf16[160,1176]{1,0:T(8,128)(2,1)S(1)}, bf16[160,1176]{1,0:T(8,128)(2,1)}, u32[]{:S(2)}, u32[]{:S(2)}) collective-permute-start(bf16[160,1176]{1,0:T(8,128)(2,1)S(1)} %collective-permute-done.2.refs_1_), channel_id=1, source_target_pairs={{0,16},{16,0},{1,17},{17,1},{2,18},{18,2},{3,19},{19,3},{4,20},{20... | collective-permute-start | bytes 1128968 | tf_op jit(solution)/shard_map/ppermute | solution.py:445
  54.0 2.5 %collective-permute-start.6 = (bf16[160,1176]{1,0:T(8,128)(2,1)S(1)}, bf16[160,1176]{1,0:T(8,128)(2,1)}, u32[]{:S(2)}, u32[]{:S(2)}) collective-permute-start(bf16[160,1176]{1,0:T(8,128)(2,1)S(1)} %collective-permute-done.3.refs_2_), channel_id=1, source_target_pairs={{0,16},{16,0},{1,17},{17,1},{2,18},{18,2},{3,19},{19,3},{4,20},{20... | collective-permute-start | bytes 1128968 | tf_op jit(solution)/shard_map/ppermute | solution.py:445
  93.3 4.1 %collective-permute-start.7 = (bf16[512,1280]{1,0:T(8,128)(2,1)S(1)}, bf16[512,1280]{1,0:T(8,128)(2,1)S(1)}, u32[]{:S(2)}, u32[]{:S(2)}) collective-permute-start(bf16[512,1280]{1,0:T(8,128)(2,1)S(1)} %get-tuple-element.26.grad0_ref), channel_id=1, source_target_pairs={{0,16},{16,0},{1,17},{17,1},{2,18},{18,2},{3,19},{19,3},{4,20},{20... | collective-permute-start | bytes 3932168 | tf_op jit(solution)/shard_map/ppermute | solution.py:452
  93.4 4.0 %collective-permute-start.8 = (bf16[512,640]{1,0:T(8,128)(2,1)S(1)}, bf16[512,640]{1,0:T(8,128)(2,1)S(1)}, u32[]{:S(2)}, u32[]{:S(2)}) collective-permute-start(bf16[512,640]{1,0:T(8,128)(2,1)S(1)} %get-tuple-element.28), channel_id=1, source_target_pairs={{0,16},{16,0},{1,17},{17,1},{2,18},{18,2},{3,19},{19,3},{4,20},{20... | collective-permute-start | bytes 1966088 | tf_op jit(solution)/shard_map/ppermute | solution.py:451
  100.5 8.4 %collective-permute-start.9 = (bf16[1600,128]{1,0:T(8,128)(2,1)S(1)}, bf16[1600,128]{1,0:T(8,128)(2,1)S(1)}, u32[]{:S(2)}, u32[]{:S(2)}) collective-permute-start(bf16[1600,128]{1,0:T(8,128)(2,1)S(1)} %get-tuple-element.31), channel_id=1, source_target_pairs={{0,1},{16,20},{1,2},{17,21},{2,3},{18,22},{3,0},{19,23},{4,5},{20,... | collective-permute-start | bytes 1228808 | tf_op jit(solution)/shard_map/ppermute | solution.py:454
  101.8 10.9 %collective-permute-start.10 = (bf16[1600,128]{1,0:T(8,128)(2,1)S(1)}, bf16[1600,128]{1,0:T(8,128)(2,1)S(1)}, u32[]{:S(2)}, u32[]{:S(2)}) collective-permute-start(bf16[1600,128]{1,0:T(8,128)(2,1)S(1)} %get-tuple-element.32), channel_id=1, source_target_pairs={{0,3},{16,28},{1,0},{17,29},{2,1},{18,30},{3,2},{19,31},{4,7},{20,... | collective-permute-start | bytes 1228808 | tf_op jit(solution)/shard_map/ppermute | solution.py:454
  103.3 10.6 %collective-permute-start.11 = (bf16[1600,128]{1,0:T(8,128)(2,1)S(1)}, bf16[1600,128]{1,0:T(8,128)(2,1)S(1)}, u32[]{:S(2)}, u32[]{:S(2)}) collective-permute-start(bf16[1600,128]{1,0:T(8,128)(2,1)S(1)} %get-tuple-element.33), channel_id=1, source_target_pairs={{0,2},{16,24},{1,3},{17,25},{2,0},{18,26},{3,1},{19,27},{4,6},{20,... | collective-permute-start | bytes 1228808 | tf_op jit(solution)/shard_map/ppermute | solution.py:454
  114.7 5.1 %collective-permute-start.12 = (bf16[400,128]{1,0:T(8,128)(2,1)S(1)}, bf16[400,128]{1,0:T(8,128)(2,1)S(1)}, u32[]{:S(2)}, u32[]{:S(2)}) collective-permute-start(bf16[400,128]{1,0:T(8,128)(2,1)S(1)} %get-tuple-element.35), channel_id=1, source_target_pairs={{0,4},{16,17},{1,5},{17,18},{2,6},{18,19},{3,7},{19,16},{4,8},{20,... | collective-permute-start | bytes 307208 | tf_op jit(solution)/shard_map/ppermute | solution.py:456
  114.8 5.4 %collective-permute-start.13 = (bf16[400,128]{1,0:T(8,128)(2,1)S(1)}, bf16[400,128]{1,0:T(8,128)(2,1)S(1)}, u32[]{:S(2)}, u32[]{:S(2)}) collective-permute-start(bf16[400,128]{1,0:T(8,128)(2,1)S(1)} %get-tuple-element.36), channel_id=1, source_target_pairs={{0,12},{16,19},{1,13},{17,16},{2,14},{18,17},{3,15},{19,18},{4,0},... | collective-permute-start | bytes 307208 | tf_op jit(solution)/shard_map/ppermute | solution.py:456
  117.5 5.0 %collective-permute-start.14 = (bf16[400,128]{1,0:T(8,128)(2,1)S(1)}, bf16[400,128]{1,0:T(8,128)(2,1)S(1)}, u32[]{:S(2)}, u32[]{:S(2)}) collective-permute-start(bf16[400,128]{1,0:T(8,128)(2,1)S(1)} %get-tuple-element.37), channel_id=1, source_target_pairs={{0,8},{16,18},{1,9},{17,19},{2,10},{18,16},{3,11},{19,17},{4,12},{... | collective-permute-start | bytes 307208 | tf_op jit(solution)/shard_map/ppermute | solution.py:456
  146.0 8.1 %collective-permute-start.17 = (f32[400,128]{1,0:T(8,128)S(1)}, f32[400,128]{1,0:T(8,128)S(1)}, u32[]{:S(2)}, u32[]{:S(2)}) collective-permute-start(f32[400,128]{1,0:T(8,128)S(1)} %slice.8.refs_0_), channel_id=1, source_target_pairs={{0,12},{4,0},{8,4},{12,8},{1,13},{5,1},{9,5},{13,9},{2,14},{6,2},{... | collective-permute-start | bytes 614408 | tf_op jit(solution)/shard_map/ppermute | solution.py:461
  148.9 9.7 %collective-permute-start.16 = (f32[400,128]{1,0:T(8,128)S(1)}, f32[400,128]{1,0:T(8,128)S(1)}, u32[]{:S(2)}, u32[]{:S(2)}) collective-permute-start(f32[400,128]{1,0:T(8,128)S(1)} %slice.8.refs_0_), channel_id=1, source_target_pairs={{0,8},{4,12},{8,0},{12,4},{1,9},{5,13},{9,1},{13,5},{2,10},{6,14},... | collective-permute-start | bytes 614408 | tf_op jit(solution)/shard_map/ppermute | solution.py:461
  149.4 10.9 %collective-permute-start.15 = (f32[400,128]{1,0:T(8,128)S(1)}, f32[400,128]{1,0:T(8,128)S(1)}, u32[]{:S(2)}, u32[]{:S(2)}) collective-permute-start(f32[400,128]{1,0:T(8,128)S(1)} %slice.8.refs_0_), channel_id=1, source_target_pairs={{0,4},{4,8},{8,12},{12,0},{1,5},{5,9},{9,13},{13,1},{2,6},{6,10},{... | collective-permute-start | bytes 614408 | tf_op jit(solution)/shard_map/ppermute | solution.py:461
  149.6 12.8 %collective-permute-start.18 = (f32[400,128]{1,0:T(8,128)S(1)}, f32[400,128]{1,0:T(8,128)S(1)}, u32[]{:S(2)}, u32[]{:S(2)}) collective-permute-start(f32[400,128]{1,0:T(8,128)S(1)} %slice.8.refs_0_), channel_id=1, source_target_pairs={{0,16},{16,0},{1,17},{17,1},{2,18},{18,2},{3,19},{19,3},{4,20},{20... | collective-permute-start | bytes 614408 | tf_op jit(solution)/shard_map/ppermute | solution.py:462
  154.0 8.4 %collective-permute-start.21 = (f32[400,128]{1,0:T(8,128)S(1)}, f32[400,128]{1,0:T(8,128)S(1)}, u32[]{:S(2)}, u32[]{:S(2)}) collective-permute-start(f32[400,128]{1,0:T(8,128)S(1)} %collective-permute-done.17.refs_3_), channel_id=1, source_target_pairs={{0,16},{16,0},{1,17},{17,1},{2,18},{18,2},{3,19},{19,3},{4,20},{20... | collective-permute-start | bytes 614408 | tf_op jit(solution)/shard_map/ppermute | solution.py:462
  158.6 3.8 %collective-permute-start.20 = (f32[400,128]{1,0:T(8,128)S(1)}, f32[400,128]{1,0:T(8,128)S(1)}, u32[]{:S(2)}, u32[]{:S(2)}) collective-permute-start(f32[400,128]{1,0:T(8,128)S(1)} %collective-permute-done.16.refs_2_), channel_id=1, source_target_pairs={{0,16},{16,0},{1,17},{17,1},{2,18},{18,2},{3,19},{19,3},{4,20},{20... | collective-permute-start | bytes 614408 | tf_op jit(solution)/shard_map/ppermute | solution.py:462
  160.3 3.2 %collective-permute-start.19 = (f32[400,128]{1,0:T(8,128)S(1)}, f32[400,128]{1,0:T(8,128)S(1)}, u32[]{:S(2)}, u32[]{:S(2)}) collective-permute-start(f32[400,128]{1,0:T(8,128)S(1)} %collective-permute-done.15.refs_1_), channel_id=1, source_target_pairs={{0,16},{16,0},{1,17},{17,1},{2,18},{18,2},{3,19},{19,3},{4,20},{20... | collective-permute-start | bytes 614408 | tf_op jit(solution)/shard_map/ppermute | solution.py:462
  (10 other events, 122.6 us)
where the time goes:
time: 167 us; the launch traced here: 166 us
  waiting for transfers between devices  50 us (30%)
  starting transfers between devices  46.3 us (28%)
  Pallas kernels  43.2 us (26%)
  blocking collectives  23.3 us (14%)
  local copies, waits for them, and re-layouts  2.64 us (2%)
    ppermute x4, starting transfers between devices, shards(): lax.ppermute(part, 'core', swap)  12.8 us
    all_to_all x1, blocking collectives, shards(): lax.all_to_all(quarter.reshape(8, PIECE, 128), 'z', 0, 0, tiled=True)  11.9 us
    all_to_all x1, blocking collectives, copies(): return lax.all_to_all(array, axis, 0, 0, tiled=True)  11.4 us
    all_to_all x1, waiting for transfers between devices, shards(): arrived1 = lax.all_to_all(packed1, ('z', 'core'), 0, 0, tiled=True)  11.1 us
    pallas_call x2, Pallas kernels, packed_rows(): pl.pallas_call(patch_kernel, out_shape=jax.ShapeDtypeStruct(shape, jnp.bf...  10.8 us
    all_to_all x1, starting transfers between devices, shards(): arrived0 = lax.all_to_all(packed0, ('z', 'core'), 0, 0, tiled=True)  10.1 us
    ppermute x3, waiting for transfers between devices, shards(): parts = [lax.ppermute(part, 'fsdp', ring(by)) for by in (1, 2, 3)]  9.68 us
    ppermute x3, waiting for transfers between devices, shards(): lax.ppermute(sent[by - 1], plane, plane_shift(by, 0))  9.17 us
  transfers between devices with their start and end apart: 24, of which 15 were waited for; matrix products, arithmetic and copies ran while one was open for 2% of the time, Pallas kernels for 14%

commit v1 on v0

--- a/solution.py
+++ b/solution.py
@@ -28,7 +28,7 @@
 QUARTER = LINE // 4
 STEP = 80
 PIECE = 56
-BLOCK = 128
+BLOCK = 256
 SUMS = 96
 ALL = pl.BlockSpec(memory_space=pltpu.VMEM)
 FAR = pl.BlockSpec(memory_space=pltpu.HBM)
@@ -70,7 +70,7 @@
         for c in range(COLOURS):
             wide = dot(ref[0, 0, 0, c], spread)
             for h in range(2):
-                spread_ref[k, c, h] = wide[:, h * 128 : (h + 1) * 128]
+                spread_ref[k, c, h, :SIDE] = wide[:, h * 128 : (h + 1) * 128]
 
     @pl.when(valid_ref[0] == 0)
     def _():
@@ -128,7 +128,7 @@
         ],
         out_specs=pl.BlockSpec(shape, lambda i: (0, 0, 0)),
         scratch_shapes=[
-            pltpu.VMEM((2, COLOURS, 2, SIDE, 128), jnp.float32),
+            pltpu.VMEM((2, COLOURS, 2, GH * (PS + 1), 128), jnp.float32),
             pltpu.VMEM((ROWS, HALF), jnp.bfloat16),
         ],
         compiler_params=WIDE,
@@ -227,10 +227,13 @@
         send_ref[...] = part_ref[:, D:].astype(jnp.bfloat16)
 
     sums_ref[...] = jnp.zeros_like(sums_ref)
+    for i in range(D // 256):
+        at = slice(i * 256, (i + 1) * 256)
+        part_ref[:, at] += dot(rows1_ref[...], w_ref[at, :], LANES)
 
     def block(i, carry):
         here = pl.ds(pl.multiple_of(i * BLOCK, BLOCK), BLOCK)
-        embedded = part_ref[here, :D] + dot(rows1_ref[here, :], w_ref[...], LANES)
+        embedded = part_ref[here, :D]
         deviation = embedded - jnp.mean(embedded, axis=-1, keepdims=True)
         variance = jnp.mean(deviation * deviation, axis=-1, keepdims=True)
         inverse_std = lax.rsqrt(variance + 1e-06)

time: 167 us -> 165 us (0.988)
  no operation moved by 1% of the time
where the time goes in v1:
time: 165 us
  waiting for transfers between devices  50 us (30%)
  starting transfers between devices  46.2 us (28%)
  Pallas kernels  42 us (25%)
  blocking collectives  23.3 us (14%)
  local copies, waits for them, and re-layouts  2.64 us (2%)
    ppermute x4, starting transfers between devices, shards(): lax.ppermute(part, 'core', swap)  12.9 us
    all_to_all x1, blocking collectives, shards(): lax.all_to_all(quarter.reshape(8, PIECE, 128), 'z', 0, 0, tiled=True)  11.9 us
    all_to_all x1, blocking collectives, copies(): return lax.all_to_all(array, axis, 0, 0, tiled=True)  11.4 us
    all_to_all x1, waiting for transfers between devices, shards(): arrived1 = lax.all_to_all(packed1, ('z', 'core'), 0, 0, tiled=True)  11.1 us
    pallas_call x2, Pallas kernels, packed_rows(): pl.pallas_call(patch_kernel, out_shape=jax.ShapeDtypeStruct(shape, jnp.bf...  10.8 us
    all_to_all x1, starting transfers between devices, shards(): arrived0 = lax.all_to_all(packed0, ('z', 'core'), 0, 0, tiled=True)  10.1 us
    ppermute x3, waiting for transfers between devices, shards(): parts = [lax.ppermute(part, 'fsdp', ring(by)) for by in (1, 2, 3)]  9.68 us
    ppermute x3, waiting for transfers between devices, shards(): lax.ppermute(sent[by - 1], plane, plane_shift(by, 0))  9.18 us
  transfers between devices with their start and end apart: 24, of which 15 were waited for; matrix products, arithmetic and copies ran while one was open for 2% of the time, Pallas kernels for 14%

profile of v1, /device:TPU:1, one launch (start us, length us, event | category | flops | bytes accessed | tf_op | source)
XLA Modules:
  0.0 165.0 jit_solution(14605803199142464758)
XLA Ops:
  0.6 5.3 %patch_rows.2 = bf16[16,296,128]{2,1,0:T(8,128)(2,1)} custom-call(s32[1]{0:T(128)} %constant.22.clone.1.valid_ref, s32[1,512]{1,0:T(1,128)} %bitcast.12, bf16[1,1,4,3,224,224]{5,4,3,2,1,0:T(8,128)(2,1)} %fb_ref.3, bf16[1,1,4,3,224,224]{5,4,3,2,1,0:T(8,128)(2,1)} %fb_ref.3), custom_call_target="tpu_custom_call" | custom-call | tf_op jit(solution)/shard_map/patch_rows/pallas_call | solution.py:119
  6.0 10.1 %all-to-all-start.1 = ((bf16[16,296,128]{2,1,0:T(8,128)(2,1)}), bf16[16,296,128]{2,1,0:T(8,128)(2,1)S(1)}, u32[]{:S(2)}, u32[]{:S(2)}) async-start(bf16[16,296,128]{2,1,0:T(8,128)(2,1)} %patch_rows.2), calls=%async_computation.1 | async-start | bytes 2424832 | tf_op jit(solution)/shard_map/all_to_all | solution.py:441
  16.1 2.8 %collective-permute-start.3 = (bf16[160,1176]{1,0:T(8,128)(2,1)S(1)}, bf16[160,1176]{1,0:T(8,128)(2,1)S(1)}, u32[]{:S(2)}, u32[]{:S(2)}) collective-permute-start(bf16[160,1176]{1,0:T(8,128)(2,1)S(1)} %constant_dynamic-slice_fusion), channel_id=1, source_target_pairs={{0,3},{1,0},{2,1},{3,2},{4,7},{5,4},{6,5},{7,6},{8,11},{9,8},{10,9... | collective-permute-start | bytes 1128968 | tf_op jit(solution)/shard_map/ppermute | solution.py:444
  22.3 8.7 %collective-permute-done.fa_ref = bf16[1,1,1,3,224,224]{5,4,3,2,1,0:T(8,128)(2,1)S(1)} collective-permute-done((bf16[1,1,1,3,224,224]{5,4,3,2,1,0:T(8,128)(2,1)S(1)}, bf16[1,1,1,3,224,224]{5,4,3,2,1,0:T(8,128)(2,1)S(1)}, u32[]{:S(2)}, u32[]{:S(2)}) %collective-permute-start) | collective-permute-done | bytes 301088 | tf_op jit(solution)/shard_map/ppermute | solution.py:436
  31.0 5.5 %collective-permute-done.3.refs_2_ = bf16[160,1176]{1,0:T(8,128)(2,1)S(1)} collective-permute-done((bf16[160,1176]{1,0:T(8,128)(2,1)S(1)}, bf16[160,1176]{1,0:T(8,128)(2,1)S(1)}, u32[]{:S(2)}, u32[]{:S(2)}) %collective-permute-start.3) | collective-permute-done | bytes 376352 | tf_op jit(solution)/shard_map/ppermute | solution.py:444
  36.4 4.2 %collective-permute-done.1.refs_0_ = bf16[160,1176]{1,0:T(8,128)(2,1)S(1)} collective-permute-done((bf16[160,1176]{1,0:T(8,128)(2,1)S(1)}, bf16[160,1176]{1,0:T(8,128)(2,1)S(1)}, u32[]{:S(2)}, u32[]{:S(2)}) %collective-permute-start.1) | collective-permute-done | bytes 376352 | tf_op jit(solution)/shard_map/ppermute | solution.py:444
  40.7 5.5 %patch_rows.3 = bf16[16,296,128]{2,1,0:T(8,128)(2,1)} custom-call(s32[1]{0:T(128)} %bitcast.6.valid_ref, s32[1,512]{1,0:T(1,128)} %bitcast.13, bf16[1,1,1,3,224,224]{5,4,3,2,1,0:T(8,128)(2,1)} %copy-done.7, bf16[1,1,4,3,224,224]{5,4,3,2,1,0:T(8,128)(2,1)} %fb_ref.3), custom_call_target="tpu_custom_call" | custom-call | tf_op jit(solution)/shard_map/patch_rows/pallas_call | solution.py:119
  47.3 6.2 %all-to-all-start = ((bf16[16,296,128]{2,1,0:T(8,128)(2,1)}), bf16[16,296,128]{2,1,0:T(8,128)(2,1)S(1)}, u32[]{:S(2)}, u32[]{:S(2)}) async-start(bf16[16,296,128]{2,1,0:T(8,128)(2,1)} %patch_rows.3), calls=%async_computation | async-start | bytes 2424832 | tf_op jit(solution)/shard_map/all_to_all | solution.py:447
  56.6 9.1 %weight_columns.1.w_ref.w_far = bf16[1280,1280]{1,0:T(8,128)(2,1)} custom-call(s32[5]{0:T(128)} %stack.23.place_ref.core_ref, s32[1,1176]{1,0:T(1,128)} %constant.26.clone.column_ref, bf16[320,1176]{1,0:T(8,128)(2,1)} %own_ref.1, bf16[160,1176]{1,0:T(8,128)(2,1)} %copy-done.6, bf16[160,1176]{1,0:T(8,128)(2,1)} %copy-done.5, bf16[160,1176]{1,0:T(8,128)(2,1)} %copy-done.4, ...), custom_call_target="tpu_custom_call" | custom-call | tf_op jit(solution)/shard_map/weight_columns/pallas_call | solution.py:154
  65.6 8.0 %first_half.1.part_far = f32[512,1920]{1,0:T(8,128)} custom-call(s32[512,1]{1,0:T(8,128)} %copy.11.slot_ref, bf16[16,296,128]{2,1,0:T(8,128)(2,1)} %copy-done.2, bf16[1280,1280]{1,0:T(8,128)(2,1)} %weight_columns.1.w_ref.w_far), custom_call_target="tpu_custom_call" | custom-call | tf_op jit(solution)/shard_map/first_half/pallas_call | solution.py:192
  73.7 11.1 %all-to-all-done.arr_ref = bf16[16,296,128]{2,1,0:T(8,128)(2,1)S(1)} async-done(((bf16[16,296,128]{2,1,0:T(8,128)(2,1)}), bf16[16,296,128]{2,1,0:T(8,128)(2,1)S(1)}, u32[]{:S(2)}, u32[]{:S(2)}) %all-to-all-start) | async-done | bytes 1212448 | tf_op jit(solution)/shard_map/all_to_all | solution.py:447
  84.7 7.4 %norm_backward.1 = (bf16[512,1280]{1,0:T(8,128)(2,1)S(1)}, bf16[512,640]{1,0:T(8,128)(2,1)S(1)}, bf16[512,640]{1,0:T(8,128)(2,1)S(1)}, f32[16,1280]{1,0:T(8,128)S(1)}) custom-call(s32[5]{0:T(128)S(1)} %copy-done.1, s32[512,1]{1,0:T(8,128)S(1)} %copy-done, bf16[16,296,128]{2,1,0:T(8,128)(2,1)S(1)} %all-to-all-done.arr_ref, f32[512,1920]{1,0:T(8,128)} %first_half.1.part_far, ...), custom_call_target="tpu_custom_call" | custom-call | tf_op jit(solution)/shard_map/norm_backward/pallas_call | solution.py:258
  92.7 3.5 %collective-permute-done.8.rows1_ref = bf16[512,640]{1,0:T(8,128)(2,1)S(1)} collective-permute-done((bf16[512,640]{1,0:T(8,128)(2,1)S(1)}, bf16[512,640]{1,0:T(8,128)(2,1)S(1)}, u32[]{:S(2)}, u32[]{:S(2)}) %collective-permute-start.8) | collective-permute-done | bytes 655392 | tf_op jit(solution)/shard_map/ppermute | solution.py:454
  96.2 3.2 %products.1 = (f32[1600,128]{1,0:T(8,128)S(1)}, bf16[1600,128]{1,0:T(8,128)(2,1)S(1)}, bf16[1600,128]{1,0:T(8,128)(2,1)S(1)}, bf16[1600,128]{1,0:T(8,128)(2,1)S(1)}) custom-call(s32[5]{0:T(128)S(1)} %copy-done.1, bf16[512,1280]{1,0:T(8,128)(2,1)S(1)} %get-tuple-element.26.grad0_ref, bf16[512,1280]{1,0:T(8,128)(2,1)S(1)} %collective-permute-done.7.grad1_ref, ...), custom_call_target="tpu_custom_call" | custom-call | tf_op jit(solution)/shard_map/products/pallas_call | solution.py:310
  103.6 4.1 %collective-permute-done.9.in1_ref = bf16[1600,128]{1,0:T(8,128)(2,1)S(1)} collective-permute-done((bf16[1600,128]{1,0:T(8,128)(2,1)S(1)}, bf16[1600,128]{1,0:T(8,128)(2,1)S(1)}, u32[]{:S(2)}, u32[]{:S(2)}) %collective-permute-start.9) | collective-permute-done | bytes 409632 | tf_op jit(solution)/shard_map/ppermute | solution.py:457
  107.8 3.7 %collective-permute-done.10.in2_ref = bf16[1600,128]{1,0:T(8,128)(2,1)S(1)} collective-permute-done((bf16[1600,128]{1,0:T(8,128)(2,1)S(1)}, bf16[1600,128]{1,0:T(8,128)(2,1)S(1)}, u32[]{:S(2)}, u32[]{:S(2)}) %collective-permute-start.10) | collective-permute-done | bytes 409632 | tf_op jit(solution)/shard_map/ppermute | solution.py:457
  113.7 2.7 %collective-permute-start.13 = (bf16[400,128]{1,0:T(8,128)(2,1)S(1)}, bf16[400,128]{1,0:T(8,128)(2,1)S(1)}, u32[]{:S(2)}, u32[]{:S(2)}) collective-permute-start(bf16[400,128]{1,0:T(8,128)(2,1)S(1)} %get-tuple-element.36), channel_id=1, source_target_pairs={{0,12},{16,19},{1,13},{17,16},{2,14},{18,17},{3,15},{19,18},{4,0},... | collective-permute-start | bytes 307208 | tf_op jit(solution)/shard_map/ppermute | solution.py:459
  116.4 2.3 %collective-permute-done.12 = bf16[400,128]{1,0:T(8,128)(2,1)S(1)} collective-permute-done((bf16[400,128]{1,0:T(8,128)(2,1)S(1)}, bf16[400,128]{1,0:T(8,128)(2,1)S(1)}, u32[]{:S(2)}, u32[]{:S(2)}) %collective-permute-start.12) | collective-permute-done | bytes 102432 | tf_op jit(solution)/shard_map/ppermute | solution.py:459
  121.5 11.9 %all_to_all.20 = f32[8,56,128]{2,1,0:T(8,128)S(1)} all-to-all(f32[8,56,128]{2,1,0:T(8,128)S(1)} %bitcast.10), channel_id=1, replica_groups=mesh['z'=8,'core'=2,'slab'=4,'fsdp'=4] {'z'}, dimensions={0} | all-to-all | bytes 458752 | tf_op jit(solution)/shard_map/all_to_all | solution.py:462
  133.4 11.4 %all_to_all.21 = f32[8,56,128]{2,1,0:T(8,128)S(1)} all-to-all(f32[8,56,128]{2,1,0:T(8,128)S(1)} %broadcast_in_dim.13), channel_id=1, replica_groups=mesh['z'=8,'core'=2,'slab'=4,'fsdp'=4] {'z'}, dimensions={0} | all-to-all | bytes 458752 | tf_op jit(solution)/shard_map/all_to_all | solution.py:427
  144.9 2.8 %collective-permute-start.17 = (f32[400,128]{1,0:T(8,128)S(1)}, f32[400,128]{1,0:T(8,128)S(1)}, u32[]{:S(2)}, u32[]{:S(2)}) collective-permute-start(f32[400,128]{1,0:T(8,128)S(1)} %slice.8.refs_0_), channel_id=1, source_target_pairs={{0,12},{4,0},{8,4},{12,8},{1,13},{5,1},{9,5},{13,9},{2,14},{6,2},{... | collective-permute-start | bytes 614408 | tf_op jit(solution)/shard_map/ppermute | solution.py:464
  148.3 4.6 %collective-permute-start.18 = (f32[400,128]{1,0:T(8,128)S(1)}, f32[400,128]{1,0:T(8,128)S(1)}, u32[]{:S(2)}, u32[]{:S(2)}) collective-permute-start(f32[400,128]{1,0:T(8,128)S(1)} %slice.8.refs_0_), channel_id=1, source_target_pairs={{0,16},{16,0},{1,17},{17,1},{2,18},{18,2},{3,19},{19,3},{4,20},{20... | collective-permute-start | bytes 614408 | tf_op jit(solution)/shard_map/ppermute | solution.py:465
  152.9 4.4 %collective-permute-start.21 = (f32[400,128]{1,0:T(8,128)S(1)}, f32[400,128]{1,0:T(8,128)S(1)}, u32[]{:S(2)}, u32[]{:S(2)}) collective-permute-start(f32[400,128]{1,0:T(8,128)S(1)} %collective-permute-done.17.refs_3_), channel_id=1, source_target_pairs={{0,16},{16,0},{1,17},{17,1},{2,18},{18,2},{3,19},{19,3},{4,20},{20... | collective-permute-start | bytes 614408 | tf_op jit(solution)/shard_map/ppermute | solution.py:465
  162.3 2.7 %column_order.1 = (f32[320,1176]{1,0:T(8,128)}, f32[2,320]{1,0:T(2,128)}) custom-call(s32[5]{0:T(128)S(1)} %copy-done.1, f32[400,128]{1,0:T(8,128)S(1)} %slice.8.refs_0_, f32[400,128]{1,0:T(8,128)S(1)} %collective-permute-done.15.refs_1_, f32[400,128]{1,0:T(8,128)S(1)} %collective-permute-done.16.refs_2_, f32[400,128]{1,0:T(8,128)S(1)} %collective-permute-done.17.refs_3_, ...), custom_call_target="tpu_custom_call" | custom-call | tf_op jit(solution)/shard_map/column_order/pallas_call | solution.py:390
  (64 shorter events, 23.1 us)
Async XLA Ops:
  6.0 41.3 %all-to-all-start.1 = ((bf16[16,296,128]{2,1,0:T(8,128)(2,1)}), bf16[16,296,128]{2,1,0:T(8,128)(2,1)S(1)}, u32[]{:S(2)}, u32[]{:S(2)}) async-start(bf16[16,296,128]{2,1,0:T(8,128)(2,1)} %patch_rows.2), calls=%async_computation.1 | async-start | bytes 2424832 | tf_op jit(solution)/shard_map/all_to_all | solution.py:441
  16.1 20.3 %collective-permute-start.3 = (bf16[160,1176]{1,0:T(8,128)(2,1)S(1)}, bf16[160,1176]{1,0:T(8,128)(2,1)S(1)}, u32[]{:S(2)}, u32[]{:S(2)}) collective-permute-start(bf16[160,1176]{1,0:T(8,128)(2,1)S(1)} %constant_dynamic-slice_fusion), channel_id=1, source_target_pairs={{0,3},{1,0},{2,1},{3,2},{4,7},{5,4},{6,5},{7,6},{8,11},{9,8},{10,9... | collective-permute-start | bytes 1128968 | tf_op jit(solution)/shard_map/ppermute | solution.py:444
  19.0 17.4 %collective-permute-start.2 = (bf16[160,1176]{1,0:T(8,128)(2,1)S(1)}, bf16[160,1176]{1,0:T(8,128)(2,1)S(1)}, u32[]{:S(2)}, u32[]{:S(2)}) collective-permute-start(bf16[160,1176]{1,0:T(8,128)(2,1)S(1)} %constant_dynamic-slice_fusion), channel_id=1, source_target_pairs={{0,2},{1,3},{2,0},{3,1},{4,6},{5,7},{6,4},{7,5},{8,10},{9,11},{10,... | collective-permute-start | bytes 1128968 | tf_op jit(solution)/shard_map/ppermute | solution.py:444
  19.3 21.3 %collective-permute-start.1 = (bf16[160,1176]{1,0:T(8,128)(2,1)S(1)}, bf16[160,1176]{1,0:T(8,128)(2,1)S(1)}, u32[]{:S(2)}, u32[]{:S(2)}) collective-permute-start(bf16[160,1176]{1,0:T(8,128)(2,1)S(1)} %constant_dynamic-slice_fusion), channel_id=1, source_target_pairs={{0,1},{1,2},{2,3},{3,0},{4,5},{5,6},{6,7},{7,4},{8,9},{9,10},{10,1... | collective-permute-start | bytes 1128968 | tf_op jit(solution)/shard_map/ppermute | solution.py:444
  21.0 9.9 %collective-permute-start = (bf16[1,1,1,3,224,224]{5,4,3,2,1,0:T(8,128)(2,1)S(1)}, bf16[1,1,1,3,224,224]{5,4,3,2,1,0:T(8,128)(2,1)S(1)}, u32[]{:S(2)}, u32[]{:S(2)}) collective-permute-start(bf16[1,1,1,3,224,224]{5,4,3,2,1,0:T(8,128)(2,1)S(1)} %slice.6), channel_id=1, source_target_pairs={{0,4},{4,8},{8,12},{12,0},{1,5},{5,9},{9,13},{13,1},{2,6},{6,10},{... | collective-permute-start | bytes 903176 | tf_op jit(solution)/shard_map/ppermute | solution.py:436
  47.3 37.4 %all-to-all-start = ((bf16[16,296,128]{2,1,0:T(8,128)(2,1)}), bf16[16,296,128]{2,1,0:T(8,128)(2,1)S(1)}, u32[]{:S(2)}, u32[]{:S(2)}) async-start(bf16[16,296,128]{2,1,0:T(8,128)(2,1)} %patch_rows.3), calls=%async_computation | async-start | bytes 2424832 | tf_op jit(solution)/shard_map/all_to_all | solution.py:447
  53.5 2.3 %collective-permute-start.4 = (bf16[160,1176]{1,0:T(8,128)(2,1)}, bf16[160,1176]{1,0:T(8,128)(2,1)}, u32[]{:S(2)}, u32[]{:S(2)}) collective-permute-start(bf16[160,1176]{1,0:T(8,128)(2,1)} %copy-done.6), channel_id=1, source_target_pairs={{0,16},{16,0},{1,17},{17,1},{2,18},{18,2},{3,19},{19,3},{4,20},{20... | collective-permute-start | bytes 1128968 | tf_op jit(solution)/shard_map/ppermute | solution.py:448
  53.7 2.3 %collective-permute-start.5 = (bf16[160,1176]{1,0:T(8,128)(2,1)S(1)}, bf16[160,1176]{1,0:T(8,128)(2,1)}, u32[]{:S(2)}, u32[]{:S(2)}) collective-permute-start(bf16[160,1176]{1,0:T(8,128)(2,1)S(1)} %collective-permute-done.2.refs_1_), channel_id=1, source_target_pairs={{0,16},{16,0},{1,17},{17,1},{2,18},{18,2},{3,19},{19,3},{4,20},{20... | collective-permute-start | bytes 1128968 | tf_op jit(solution)/shard_map/ppermute | solution.py:448
  54.0 2.5 %collective-permute-start.6 = (bf16[160,1176]{1,0:T(8,128)(2,1)S(1)}, bf16[160,1176]{1,0:T(8,128)(2,1)}, u32[]{:S(2)}, u32[]{:S(2)}) collective-permute-start(bf16[160,1176]{1,0:T(8,128)(2,1)S(1)} %collective-permute-done.3.refs_2_), channel_id=1, source_target_pairs={{0,16},{16,0},{1,17},{17,1},{2,18},{18,2},{3,19},{19,3},{4,20},{20... | collective-permute-start | bytes 1128968 | tf_op jit(solution)/shard_map/ppermute | solution.py:448
  92.1 4.1 %collective-permute-start.7 = (bf16[512,1280]{1,0:T(8,128)(2,1)S(1)}, bf16[512,1280]{1,0:T(8,128)(2,1)S(1)}, u32[]{:S(2)}, u32[]{:S(2)}) collective-permute-start(bf16[512,1280]{1,0:T(8,128)(2,1)S(1)} %get-tuple-element.26.grad0_ref), channel_id=1, source_target_pairs={{0,16},{16,0},{1,17},{17,1},{2,18},{18,2},{3,19},{19,3},{4,20},{20... | collective-permute-start | bytes 3932168 | tf_op jit(solution)/shard_map/ppermute | solution.py:455
  92.2 4.0 %collective-permute-start.8 = (bf16[512,640]{1,0:T(8,128)(2,1)S(1)}, bf16[512,640]{1,0:T(8,128)(2,1)S(1)}, u32[]{:S(2)}, u32[]{:S(2)}) collective-permute-start(bf16[512,640]{1,0:T(8,128)(2,1)S(1)} %get-tuple-element.28), channel_id=1, source_target_pairs={{0,16},{16,0},{1,17},{17,1},{2,18},{18,2},{3,19},{19,3},{4,20},{20... | collective-permute-start | bytes 1966088 | tf_op jit(solution)/shard_map/ppermute | solution.py:454
  99.4 8.4 %collective-permute-start.9 = (bf16[1600,128]{1,0:T(8,128)(2,1)S(1)}, bf16[1600,128]{1,0:T(8,128)(2,1)S(1)}, u32[]{:S(2)}, u32[]{:S(2)}) collective-permute-start(bf16[1600,128]{1,0:T(8,128)(2,1)S(1)} %get-tuple-element.31), channel_id=1, source_target_pairs={{0,1},{16,20},{1,2},{17,21},{2,3},{18,22},{3,0},{19,23},{4,5},{20,... | collective-permute-start | bytes 1228808 | tf_op jit(solution)/shard_map/ppermute | solution.py:457
  100.6 10.8 %collective-permute-start.10 = (bf16[1600,128]{1,0:T(8,128)(2,1)S(1)}, bf16[1600,128]{1,0:T(8,128)(2,1)S(1)}, u32[]{:S(2)}, u32[]{:S(2)}) collective-permute-start(bf16[1600,128]{1,0:T(8,128)(2,1)S(1)} %get-tuple-element.32), channel_id=1, source_target_pairs={{0,3},{16,28},{1,0},{17,29},{2,1},{18,30},{3,2},{19,31},{4,7},{20,... | collective-permute-start | bytes 1228808 | tf_op jit(solution)/shard_map/ppermute | solution.py:457
  102.1 10.7 %collective-permute-start.11 = (bf16[1600,128]{1,0:T(8,128)(2,1)S(1)}, bf16[1600,128]{1,0:T(8,128)(2,1)S(1)}, u32[]{:S(2)}, u32[]{:S(2)}) collective-permute-start(bf16[1600,128]{1,0:T(8,128)(2,1)S(1)} %get-tuple-element.33), channel_id=1, source_target_pairs={{0,2},{16,24},{1,3},{17,25},{2,0},{18,26},{3,1},{19,27},{4,6},{20,... | collective-permute-start | bytes 1228808 | tf_op jit(solution)/shard_map/ppermute | solution.py:457
  113.6 5.1 %collective-permute-start.12 = (bf16[400,128]{1,0:T(8,128)(2,1)S(1)}, bf16[400,128]{1,0:T(8,128)(2,1)S(1)}, u32[]{:S(2)}, u32[]{:S(2)}) collective-permute-start(bf16[400,128]{1,0:T(8,128)(2,1)S(1)} %get-tuple-element.35), channel_id=1, source_target_pairs={{0,4},{16,17},{1,5},{17,18},{2,6},{18,19},{3,7},{19,16},{4,8},{20,... | collective-permute-start | bytes 307208 | tf_op jit(solution)/shard_map/ppermute | solution.py:459
  113.7 5.4 %collective-permute-start.13 = (bf16[400,128]{1,0:T(8,128)(2,1)S(1)}, bf16[400,128]{1,0:T(8,128)(2,1)S(1)}, u32[]{:S(2)}, u32[]{:S(2)}) collective-permute-start(bf16[400,128]{1,0:T(8,128)(2,1)S(1)} %get-tuple-element.36), channel_id=1, source_target_pairs={{0,12},{16,19},{1,13},{17,16},{2,14},{18,17},{3,15},{19,18},{4,0},... | collective-permute-start | bytes 307208 | tf_op jit(solution)/shard_map/ppermute | solution.py:459
  116.4 5.0 %collective-permute-start.14 = (bf16[400,128]{1,0:T(8,128)(2,1)S(1)}, bf16[400,128]{1,0:T(8,128)(2,1)S(1)}, u32[]{:S(2)}, u32[]{:S(2)}) collective-permute-start(bf16[400,128]{1,0:T(8,128)(2,1)S(1)} %get-tuple-element.37), channel_id=1, source_target_pairs={{0,8},{16,18},{1,9},{17,19},{2,10},{18,16},{3,11},{19,17},{4,12},{... | collective-permute-start | bytes 307208 | tf_op jit(solution)/shard_map/ppermute | solution.py:459
  144.9 8.1 %collective-permute-start.17 = (f32[400,128]{1,0:T(8,128)S(1)}, f32[400,128]{1,0:T(8,128)S(1)}, u32[]{:S(2)}, u32[]{:S(2)}) collective-permute-start(f32[400,128]{1,0:T(8,128)S(1)} %slice.8.refs_0_), channel_id=1, source_target_pairs={{0,12},{4,0},{8,4},{12,8},{1,13},{5,1},{9,5},{13,9},{2,14},{6,2},{... | collective-permute-start | bytes 614408 | tf_op jit(solution)/shard_map/ppermute | solution.py:464
  147.6 9.7 %collective-permute-start.16 = (f32[400,128]{1,0:T(8,128)S(1)}, f32[400,128]{1,0:T(8,128)S(1)}, u32[]{:S(2)}, u32[]{:S(2)}) collective-permute-start(f32[400,128]{1,0:T(8,128)S(1)} %slice.8.refs_0_), channel_id=1, source_target_pairs={{0,8},{4,12},{8,0},{12,4},{1,9},{5,13},{9,1},{13,5},{2,10},{6,14},... | collective-permute-start | bytes 614408 | tf_op jit(solution)/shard_map/ppermute | solution.py:464
  148.3 10.8 %collective-permute-start.15 = (f32[400,128]{1,0:T(8,128)S(1)}, f32[400,128]{1,0:T(8,128)S(1)}, u32[]{:S(2)}, u32[]{:S(2)}) collective-permute-start(f32[400,128]{1,0:T(8,128)S(1)} %slice.8.refs_0_), channel_id=1, source_target_pairs={{0,4},{4,8},{8,12},{12,0},{1,5},{5,9},{9,13},{13,1},{2,6},{6,10},{... | collective-permute-start | bytes 614408 | tf_op jit(solution)/shard_map/ppermute | solution.py:464
  148.3 12.9 %collective-permute-start.18 = (f32[400,128]{1,0:T(8,128)S(1)}, f32[400,128]{1,0:T(8,128)S(1)}, u32[]{:S(2)}, u32[]{:S(2)}) collective-permute-start(f32[400,128]{1,0:T(8,128)S(1)} %slice.8.refs_0_), channel_id=1, source_target_pairs={{0,16},{16,0},{1,17},{17,1},{2,18},{18,2},{3,19},{19,3},{4,20},{20... | collective-permute-start | bytes 614408 | tf_op jit(solution)/shard_map/ppermute | solution.py:465
  152.9 8.3 %collective-permute-start.21 = (f32[400,128]{1,0:T(8,128)S(1)}, f32[400,128]{1,0:T(8,128)S(1)}, u32[]{:S(2)}, u32[]{:S(2)}) collective-permute-start(f32[400,128]{1,0:T(8,128)S(1)} %collective-permute-done.17.refs_3_), channel_id=1, source_target_pairs={{0,16},{16,0},{1,17},{17,1},{2,18},{18,2},{3,19},{19,3},{4,20},{20... | collective-permute-start | bytes 614408 | tf_op jit(solution)/shard_map/ppermute | solution.py:465
  157.3 3.9 %collective-permute-start.20 = (f32[400,128]{1,0:T(8,128)S(1)}, f32[400,128]{1,0:T(8,128)S(1)}, u32[]{:S(2)}, u32[]{:S(2)}) collective-permute-start(f32[400,128]{1,0:T(8,128)S(1)} %collective-permute-done.16.refs_2_), channel_id=1, source_target_pairs={{0,16},{16,0},{1,17},{17,1},{2,18},{18,2},{3,19},{19,3},{4,20},{20... | collective-permute-start | bytes 614408 | tf_op jit(solution)/shard_map/ppermute | solution.py:465
  159.1 3.2 %collective-permute-start.19 = (f32[400,128]{1,0:T(8,128)S(1)}, f32[400,128]{1,0:T(8,128)S(1)}, u32[]{:S(2)}, u32[]{:S(2)}) collective-permute-start(f32[400,128]{1,0:T(8,128)S(1)} %collective-permute-done.15.refs_1_), channel_id=1, source_target_pairs={{0,16},{16,0},{1,17},{17,1},{2,18},{18,2},{3,19},{19,3},{4,20},{20... | collective-permute-start | bytes 614408 | tf_op jit(solution)/shard_map/ppermute | solution.py:465
  (10 other events, 122.6 us)

commit v2 on v1

--- a/solution.py
+++ b/solution.py
@@ -279,18 +279,34 @@
     )(core, slots, arrived, part, weight, grad_norm, grad_resid, gain)
 
 
-def product_kernel(core_ref, grad0_ref, grad1_ref, rows0_ref, rows1_ref, sums_ref, own_ref, out1_ref, out2_ref, out3_ref, terms_ref, order_ref):
-    core, place = core_ref[0], core_ref[1]
+def own_kernel(grad_ref, rows_ref, sums_ref, out_ref):
     kind = iota((128, HALF), 0)
     for i in range(D // HALF):
         here = slice(i * HALF, (i + 1) * HALF)
-        terms_ref[...] = dot(grad0_ref[:, here], rows0_ref[...], SUBLANES) + dot(
-            grad1_ref[:, here], rows1_ref[...], SUBLANES
-        )
+        out_ref[here, :] = dot(grad_ref[:, here], rows_ref[...], SUBLANES)
         gain_sum = jnp.sum(sums_ref[0:8, here], axis=0, keepdims=True)
         bias_sum = jnp.sum(sums_ref[8:16, here], axis=0, keepdims=True)
         sums = jnp.where(kind == SUMS, gain_sum, jnp.where(kind == SUMS + 1, bias_sum, 0.0))
-        terms_ref[:, HALF - 128 :] += sums.T
+        out_ref[here, HALF - 128 :] += sums.T
+
+
+def own_products(grad, rows, sums):
+    return pl.pallas_call(
+        own_kernel,
+        out_shape=jax.ShapeDtypeStruct((D, HALF), jnp.float32),
+        in_specs=[ALL] * 3,
+        out_specs=ALL,
+        compiler_params=PARAMS,
+        cost_estimate=pl.CostEstimate(flops=2 * ROWS * D * HALF, bytes_accessed=6 * 1024 * 1024, transcendentals=0),
+        name="own_products",
+    )(grad, rows, sums)
+
+
+def product_kernel(core_ref, part_ref, grad_ref, rows_ref, own_ref, out1_ref, out2_ref, out3_ref, terms_ref, order_ref):
+    core, place = core_ref[0], core_ref[1]
+    for i in range(D // HALF):
+        here = slice(i * HALF, (i + 1) * HALF)
+        terms_ref[...] = part_ref[here, :] + dot(grad_ref[:, here], rows_ref[...], SUBLANES)
         for n in range(HALF // STEP):
             y, r = divmod(i * (HALF // STEP) + n, OWNED // STEP)
             for t in range(TILES):
@@ -305,12 +321,12 @@
         ref[...] = order_ref[by + 1].astype(jnp.bfloat16)
 
 
-def products(core, grad0, grad1, rows0, rows1, sums):
+def products(core, part, grad, rows):
     sent = jax.ShapeDtypeStruct((LINE, 128), jnp.bfloat16)
     return pl.pallas_call(
         product_kernel,
         out_shape=(jax.ShapeDtypeStruct((LINE, 128), jnp.float32), sent, sent, sent),
-        in_specs=[SCALAR] + [ALL] * 5,
+        in_specs=[SCALAR] + [ALL] * 3,
         out_specs=(ALL,) * 4,
         scratch_shapes=[
             pltpu.VMEM((HALF, HALF), jnp.float32),
@@ -318,7 +334,7 @@
         ],
         compiler_params=PARAMS,
         name="products",
-    )(core, grad0, grad1, rows0, rows1, sums)
+    )(core, part, grad, rows)
 
 
 def fold_kernel(place_ref, own_ref, in1_ref, in2_ref, in3_ref, keep_ref, out1_ref, out2_ref, out3_ref, order_ref):
@@ -453,7 +469,7 @@
     )
     theirs = lax.ppermute(send, "core", swap)
     their_grads = lax.ppermute(grads, "core", swap)
-    own, *sent = products(place, grads, their_grads, mine, theirs, sums)
+    own, *sent = products(place, own_products(grads, mine, sums), their_grads, theirs)
     terms = [lax.ppermute(sent[by - 1], plane, plane_shift(by, 0)) for by in (1, 3, 2)]
     keep, *sent = fold(place, own, terms)
     terms = [lax.ppermute(sent[by - 1], plane, plane_shift(by, 1)) for by in (1, 3, 2)]

time: 165 us -> 164 us (level)
  transfers between devices with their start and end apart: 24 -> 24, of which waited for: 15 -> 15; matrix products, arithmetic and copies ran while one was open for 2% -> 2% of each run, Pallas kernels for 14% -> 15%
where the time goes in v2:
time: 164 us
  waiting for transfers between devices  48.8 us (30%)
  starting transfers between devices  46.2 us (28%)
  Pallas kernels  42.2 us (26%)
  blocking collectives  23.3 us (14%)
  local copies, waits for them, and re-layouts  2.64 us (2%)
    ppermute x4, starting transfers between devices, shards(): lax.ppermute(part, 'core', swap)  12.9 us
    all_to_all x1, blocking collectives, shards(): lax.all_to_all(quarter.reshape(8, PIECE, 128), 'z', 0, 0, tiled=True)  11.9 us
    all_to_all x1, blocking collectives, copies(): return lax.all_to_all(array, axis, 0, 0, tiled=True)  11.4 us
    all_to_all x1, waiting for transfers between devices, shards(): arrived1 = lax.all_to_all(packed1, ('z', 'core'), 0, 0, tiled=True)  11.1 us
    pallas_call x2, Pallas kernels, packed_rows(): pl.pallas_call(patch_kernel, out_shape=jax.ShapeDtypeStruct(shape, jnp.bf...  10.8 us
    all_to_all x1, starting transfers between devices, shards(): arrived0 = lax.all_to_all(packed0, ('z', 'core'), 0, 0, tiled=True)  10.1 us
    ppermute x3, waiting for transfers between devices, shards(): parts = [lax.ppermute(part, 'fsdp', ring(by)) for by in (1, 2, 3)]  9.68 us
    ppermute x3, waiting for transfers between devices, shards(): lax.ppermute(sent[by - 1], plane, plane_shift(by, 0))  9.18 us
  transfers between devices with their start and end apart: 24, of which 15 were waited for; matrix products, arithmetic and copies ran while one was open for 2% of the time, Pallas kernels for 15%

profile of v2, /device:TPU:1, one launch (start us, length us, event | category | flops | bytes accessed | tf_op | source)
XLA Modules:
  0.0 164.0 jit_solution(9991262976560095063)
XLA Ops:
  0.6 5.3 %patch_rows.2 = bf16[16,296,128]{2,1,0:T(8,128)(2,1)} custom-call(s32[1]{0:T(128)} %constant.22.clone.1.valid_ref, s32[1,512]{1,0:T(1,128)} %bitcast.12, bf16[1,1,4,3,224,224]{5,4,3,2,1,0:T(8,128)(2,1)} %fb_ref.3, bf16[1,1,4,3,224,224]{5,4,3,2,1,0:T(8,128)(2,1)} %fb_ref.3), custom_call_target="tpu_custom_call" | custom-call | tf_op jit(solution)/shard_map/patch_rows/pallas_call | solution.py:119
  6.0 10.1 %all-to-all-start.1 = ((bf16[16,296,128]{2,1,0:T(8,128)(2,1)}), bf16[16,296,128]{2,1,0:T(8,128)(2,1)S(1)}, u32[]{:S(2)}, u32[]{:S(2)}) async-start(bf16[16,296,128]{2,1,0:T(8,128)(2,1)} %patch_rows.2), calls=%async_computation.1 | async-start | bytes 2424832 | tf_op jit(solution)/shard_map/all_to_all | solution.py:457
  16.1 2.8 %collective-permute-start.3 = (bf16[160,1176]{1,0:T(8,128)(2,1)S(1)}, bf16[160,1176]{1,0:T(8,128)(2,1)S(1)}, u32[]{:S(2)}, u32[]{:S(2)}) collective-permute-start(bf16[160,1176]{1,0:T(8,128)(2,1)S(1)} %constant_dynamic-slice_fusion), channel_id=1, source_target_pairs={{0,3},{1,0},{2,1},{3,2},{4,7},{5,4},{6,5},{7,6},{8,11},{9,8},{10,9... | collective-permute-start | bytes 1128968 | tf_op jit(solution)/shard_map/ppermute | solution.py:460
  22.3 8.7 %collective-permute-done.fa_ref = bf16[1,1,1,3,224,224]{5,4,3,2,1,0:T(8,128)(2,1)S(1)} collective-permute-done((bf16[1,1,1,3,224,224]{5,4,3,2,1,0:T(8,128)(2,1)S(1)}, bf16[1,1,1,3,224,224]{5,4,3,2,1,0:T(8,128)(2,1)S(1)}, u32[]{:S(2)}, u32[]{:S(2)}) %collective-permute-start) | collective-permute-done | bytes 301088 | tf_op jit(solution)/shard_map/ppermute | solution.py:452
  31.0 5.5 %collective-permute-done.3.refs_2_ = bf16[160,1176]{1,0:T(8,128)(2,1)S(1)} collective-permute-done((bf16[160,1176]{1,0:T(8,128)(2,1)S(1)}, bf16[160,1176]{1,0:T(8,128)(2,1)S(1)}, u32[]{:S(2)}, u32[]{:S(2)}) %collective-permute-start.3) | collective-permute-done | bytes 376352 | tf_op jit(solution)/shard_map/ppermute | solution.py:460
  36.4 4.2 %collective-permute-done.1.refs_0_ = bf16[160,1176]{1,0:T(8,128)(2,1)S(1)} collective-permute-done((bf16[160,1176]{1,0:T(8,128)(2,1)S(1)}, bf16[160,1176]{1,0:T(8,128)(2,1)S(1)}, u32[]{:S(2)}, u32[]{:S(2)}) %collective-permute-start.1) | collective-permute-done | bytes 376352 | tf_op jit(solution)/shard_map/ppermute | solution.py:460
  40.7 5.5 %patch_rows.3 = bf16[16,296,128]{2,1,0:T(8,128)(2,1)} custom-call(s32[1]{0:T(128)} %bitcast.6.valid_ref, s32[1,512]{1,0:T(1,128)} %bitcast.13, bf16[1,1,1,3,224,224]{5,4,3,2,1,0:T(8,128)(2,1)} %copy-done.7, bf16[1,1,4,3,224,224]{5,4,3,2,1,0:T(8,128)(2,1)} %fb_ref.3), custom_call_target="tpu_custom_call" | custom-call | tf_op jit(solution)/shard_map/patch_rows/pallas_call | solution.py:119
  47.3 6.2 %all-to-all-start = ((bf16[16,296,128]{2,1,0:T(8,128)(2,1)}), bf16[16,296,128]{2,1,0:T(8,128)(2,1)S(1)}, u32[]{:S(2)}, u32[]{:S(2)}) async-start(bf16[16,296,128]{2,1,0:T(8,128)(2,1)} %patch_rows.3), calls=%async_computation | async-start | bytes 2424832 | tf_op jit(solution)/shard_map/all_to_all | solution.py:463
  56.6 9.1 %weight_columns.1.w_ref.w_far = bf16[1280,1280]{1,0:T(8,128)(2,1)} custom-call(s32[5]{0:T(128)} %stack.23.place_ref.core_ref, s32[1,1176]{1,0:T(1,128)} %constant.26.clone.column_ref, bf16[320,1176]{1,0:T(8,128)(2,1)} %own_ref.1, bf16[160,1176]{1,0:T(8,128)(2,1)} %copy-done.6, bf16[160,1176]{1,0:T(8,128)(2,1)} %copy-done.5, bf16[160,1176]{1,0:T(8,128)(2,1)} %copy-done.4, ...), custom_call_target="tpu_custom_call" | custom-call | tf_op jit(solution)/shard_map/weight_columns/pallas_call | solution.py:154
  65.6 8.0 %first_half.1.part_far = f32[512,1920]{1,0:T(8,128)} custom-call(s32[512,1]{1,0:T(8,128)} %copy.11.slot_ref, bf16[16,296,128]{2,1,0:T(8,128)(2,1)} %copy-done.2, bf16[1280,1280]{1,0:T(8,128)(2,1)} %weight_columns.1.w_ref.w_far), custom_call_target="tpu_custom_call" | custom-call | tf_op jit(solution)/shard_map/first_half/pallas_call | solution.py:192
  73.7 11.1 %all-to-all-done.arr_ref = bf16[16,296,128]{2,1,0:T(8,128)(2,1)S(1)} async-done(((bf16[16,296,128]{2,1,0:T(8,128)(2,1)}), bf16[16,296,128]{2,1,0:T(8,128)(2,1)S(1)}, u32[]{:S(2)}, u32[]{:S(2)}) %all-to-all-start) | async-done | bytes 1212448 | tf_op jit(solution)/shard_map/all_to_all | solution.py:463
  84.7 7.4 %norm_backward.1 = (bf16[512,1280]{1,0:T(8,128)(2,1)S(1)}, bf16[512,640]{1,0:T(8,128)(2,1)S(1)}, bf16[512,640]{1,0:T(8,128)(2,1)S(1)}, f32[16,1280]{1,0:T(8,128)S(1)}) custom-call(s32[5]{0:T(128)S(1)} %copy-done.1, s32[512,1]{1,0:T(8,128)S(1)} %copy-done, bf16[16,296,128]{2,1,0:T(8,128)(2,1)S(1)} %all-to-all-done.arr_ref, f32[512,1920]{1,0:T(8,128)} %first_half.1.part_far, ...), custom_call_target="tpu_custom_call" | custom-call | tf_op jit(solution)/shard_map/norm_backward/pallas_call | solution.py:258
  94.0 2.2 %collective-permute-done.8.rows_ref = bf16[512,640]{1,0:T(8,128)(2,1)S(1)} collective-permute-done((bf16[512,640]{1,0:T(8,128)(2,1)S(1)}, bf16[512,640]{1,0:T(8,128)(2,1)S(1)}, u32[]{:S(2)}, u32[]{:S(2)}) %collective-permute-start.8) | collective-permute-done | bytes 655392 | tf_op jit(solution)/shard_map/ppermute | solution.py:470
  102.6 4.1 %collective-permute-done.9.in1_ref = bf16[1600,128]{1,0:T(8,128)(2,1)S(1)} collective-permute-done((bf16[1600,128]{1,0:T(8,128)(2,1)S(1)}, bf16[1600,128]{1,0:T(8,128)(2,1)S(1)}, u32[]{:S(2)}, u32[]{:S(2)}) %collective-permute-start.9) | collective-permute-done | bytes 409632 | tf_op jit(solution)/shard_map/ppermute | solution.py:473
  106.8 3.7 %collective-permute-done.10.in2_ref = bf16[1600,128]{1,0:T(8,128)(2,1)S(1)} collective-permute-done((bf16[1600,128]{1,0:T(8,128)(2,1)S(1)}, bf16[1600,128]{1,0:T(8,128)(2,1)S(1)}, u32[]{:S(2)}, u32[]{:S(2)}) %collective-permute-start.10) | collective-permute-done | bytes 409632 | tf_op jit(solution)/shard_map/ppermute | solution.py:473
  112.7 2.7 %collective-permute-start.13 = (bf16[400,128]{1,0:T(8,128)(2,1)S(1)}, bf16[400,128]{1,0:T(8,128)(2,1)S(1)}, u32[]{:S(2)}, u32[]{:S(2)}) collective-permute-start(bf16[400,128]{1,0:T(8,128)(2,1)S(1)} %get-tuple-element.36), channel_id=1, source_target_pairs={{0,12},{16,19},{1,13},{17,16},{2,14},{18,17},{3,15},{19,18},{4,0},... | collective-permute-start | bytes 307208 | tf_op jit(solution)/shard_map/ppermute | solution.py:475
  115.4 2.3 %collective-permute-done.12 = bf16[400,128]{1,0:T(8,128)(2,1)S(1)} collective-permute-done((bf16[400,128]{1,0:T(8,128)(2,1)S(1)}, bf16[400,128]{1,0:T(8,128)(2,1)S(1)}, u32[]{:S(2)}, u32[]{:S(2)}) %collective-permute-start.12) | collective-permute-done | bytes 102432 | tf_op jit(solution)/shard_map/ppermute | solution.py:475
  118.1 2.3 %collective-permute-done.14 = bf16[400,128]{1,0:T(8,128)(2,1)S(1)} collective-permute-done((bf16[400,128]{1,0:T(8,128)(2,1)S(1)}, bf16[400,128]{1,0:T(8,128)(2,1)S(1)}, u32[]{:S(2)}, u32[]{:S(2)}) %collective-permute-start.14) | collective-permute-done | bytes 102432 | tf_op jit(solution)/shard_map/ppermute | solution.py:475
  120.5 11.9 %all_to_all.20 = f32[8,56,128]{2,1,0:T(8,128)S(1)} all-to-all(f32[8,56,128]{2,1,0:T(8,128)S(1)} %bitcast.10), channel_id=1, replica_groups=mesh['z'=8,'core'=2,'slab'=4,'fsdp'=4] {'z'}, dimensions={0} | all-to-all | bytes 458752 | tf_op jit(solution)/shard_map/all_to_all | solution.py:478
  132.4 11.4 %all_to_all.21 = f32[8,56,128]{2,1,0:T(8,128)S(1)} all-to-all(f32[8,56,128]{2,1,0:T(8,128)S(1)} %broadcast_in_dim.13), channel_id=1, replica_groups=mesh['z'=8,'core'=2,'slab'=4,'fsdp'=4] {'z'}, dimensions={0} | all-to-all | bytes 458752 | tf_op jit(solution)/shard_map/all_to_all | solution.py:443
  143.8 2.8 %collective-permute-start.17 = (f32[400,128]{1,0:T(8,128)S(1)}, f32[400,128]{1,0:T(8,128)S(1)}, u32[]{:S(2)}, u32[]{:S(2)}) collective-permute-start(f32[400,128]{1,0:T(8,128)S(1)} %slice.8.refs_0_), channel_id=1, source_target_pairs={{0,12},{4,0},{8,4},{12,8},{1,13},{5,1},{9,5},{13,9},{2,14},{6,2},{... | collective-permute-start | bytes 614408 | tf_op jit(solution)/shard_map/ppermute | solution.py:480
  147.3 4.6 %collective-permute-start.18 = (f32[400,128]{1,0:T(8,128)S(1)}, f32[400,128]{1,0:T(8,128)S(1)}, u32[]{:S(2)}, u32[]{:S(2)}) collective-permute-start(f32[400,128]{1,0:T(8,128)S(1)} %slice.8.refs_0_), channel_id=1, source_target_pairs={{0,16},{16,0},{1,17},{17,1},{2,18},{18,2},{3,19},{19,3},{4,20},{20... | collective-permute-start | bytes 614408 | tf_op jit(solution)/shard_map/ppermute | solution.py:481
  151.9 4.4 %collective-permute-start.21 = (f32[400,128]{1,0:T(8,128)S(1)}, f32[400,128]{1,0:T(8,128)S(1)}, u32[]{:S(2)}, u32[]{:S(2)}) collective-permute-start(f32[400,128]{1,0:T(8,128)S(1)} %collective-permute-done.17.refs_3_), channel_id=1, source_target_pairs={{0,16},{16,0},{1,17},{17,1},{2,18},{18,2},{3,19},{19,3},{4,20},{20... | collective-permute-start | bytes 614408 | tf_op jit(solution)/shard_map/ppermute | solution.py:481
  161.3 2.7 %column_order.1 = (f32[320,1176]{1,0:T(8,128)}, f32[2,320]{1,0:T(2,128)}) custom-call(s32[5]{0:T(128)S(1)} %copy-done.1, f32[400,128]{1,0:T(8,128)S(1)} %slice.8.refs_0_, f32[400,128]{1,0:T(8,128)S(1)} %collective-permute-done.15.refs_1_, f32[400,128]{1,0:T(8,128)S(1)} %collective-permute-done.16.refs_2_, f32[400,128]{1,0:T(8,128)S(1)} %collective-permute-done.17.refs_3_, ...), custom_call_target="tpu_custom_call" | custom-call | tf_op jit(solution)/shard_map/column_order/pallas_call | solution.py:406
  (65 shorter events, 24.2 us)
Async XLA Ops:
  6.0 41.3 %all-to-all-start.1 = ((bf16[16,296,128]{2,1,0:T(8,128)(2,1)}), bf16[16,296,128]{2,1,0:T(8,128)(2,1)S(1)}, u32[]{:S(2)}, u32[]{:S(2)}) async-start(bf16[16,296,128]{2,1,0:T(8,128)(2,1)} %patch_rows.2), calls=%async_computation.1 | async-start | bytes 2424832 | tf_op jit(solution)/shard_map/all_to_all | solution.py:457
  16.1 20.3 %collective-permute-start.3 = (bf16[160,1176]{1,0:T(8,128)(2,1)S(1)}, bf16[160,1176]{1,0:T(8,128)(2,1)S(1)}, u32[]{:S(2)}, u32[]{:S(2)}) collective-permute-start(bf16[160,1176]{1,0:T(8,128)(2,1)S(1)} %constant_dynamic-slice_fusion), channel_id=1, source_target_pairs={{0,3},{1,0},{2,1},{3,2},{4,7},{5,4},{6,5},{7,6},{8,11},{9,8},{10,9... | collective-permute-start | bytes 1128968 | tf_op jit(solution)/shard_map/ppermute | solution.py:460
  19.0 17.4 %collective-permute-start.2 = (bf16[160,1176]{1,0:T(8,128)(2,1)S(1)}, bf16[160,1176]{1,0:T(8,128)(2,1)S(1)}, u32[]{:S(2)}, u32[]{:S(2)}) collective-permute-start(bf16[160,1176]{1,0:T(8,128)(2,1)S(1)} %constant_dynamic-slice_fusion), channel_id=1, source_target_pairs={{0,2},{1,3},{2,0},{3,1},{4,6},{5,7},{6,4},{7,5},{8,10},{9,11},{10,... | collective-permute-start | bytes 1128968 | tf_op jit(solution)/shard_map/ppermute | solution.py:460
  19.3 21.3 %collective-permute-start.1 = (bf16[160,1176]{1,0:T(8,128)(2,1)S(1)}, bf16[160,1176]{1,0:T(8,128)(2,1)S(1)}, u32[]{:S(2)}, u32[]{:S(2)}) collective-permute-start(bf16[160,1176]{1,0:T(8,128)(2,1)S(1)} %constant_dynamic-slice_fusion), channel_id=1, source_target_pairs={{0,1},{1,2},{2,3},{3,0},{4,5},{5,6},{6,7},{7,4},{8,9},{9,10},{10,1... | collective-permute-start | bytes 1128968 | tf_op jit(solution)/shard_map/ppermute | solution.py:460
  21.0 9.9 %collective-permute-start = (bf16[1,1,1,3,224,224]{5,4,3,2,1,0:T(8,128)(2,1)S(1)}, bf16[1,1,1,3,224,224]{5,4,3,2,1,0:T(8,128)(2,1)S(1)}, u32[]{:S(2)}, u32[]{:S(2)}) collective-permute-start(bf16[1,1,1,3,224,224]{5,4,3,2,1,0:T(8,128)(2,1)S(1)} %slice.6), channel_id=1, source_target_pairs={{0,4},{4,8},{8,12},{12,0},{1,5},{5,9},{9,13},{13,1},{2,6},{6,10},{... | collective-permute-start | bytes 903176 | tf_op jit(solution)/shard_map/ppermute | solution.py:452
  47.3 37.4 %all-to-all-start = ((bf16[16,296,128]{2,1,0:T(8,128)(2,1)}), bf16[16,296,128]{2,1,0:T(8,128)(2,1)S(1)}, u32[]{:S(2)}, u32[]{:S(2)}) async-start(bf16[16,296,128]{2,1,0:T(8,128)(2,1)} %patch_rows.3), calls=%async_computation | async-start | bytes 2424832 | tf_op jit(solution)/shard_map/all_to_all | solution.py:463
  53.5 2.3 %collective-permute-start.4 = (bf16[160,1176]{1,0:T(8,128)(2,1)}, bf16[160,1176]{1,0:T(8,128)(2,1)}, u32[]{:S(2)}, u32[]{:S(2)}) collective-permute-start(bf16[160,1176]{1,0:T(8,128)(2,1)} %copy-done.6), channel_id=1, source_target_pairs={{0,16},{16,0},{1,17},{17,1},{2,18},{18,2},{3,19},{19,3},{4,20},{20... | collective-permute-start | bytes 1128968 | tf_op jit(solution)/shard_map/ppermute | solution.py:464
  53.7 2.3 %collective-permute-start.5 = (bf16[160,1176]{1,0:T(8,128)(2,1)S(1)}, bf16[160,1176]{1,0:T(8,128)(2,1)}, u32[]{:S(2)}, u32[]{:S(2)}) collective-permute-start(bf16[160,1176]{1,0:T(8,128)(2,1)S(1)} %collective-permute-done.2.refs_1_), channel_id=1, source_target_pairs={{0,16},{16,0},{1,17},{17,1},{2,18},{18,2},{3,19},{19,3},{4,20},{20... | collective-permute-start | bytes 1128968 | tf_op jit(solution)/shard_map/ppermute | solution.py:464
  54.0 2.5 %collective-permute-start.6 = (bf16[160,1176]{1,0:T(8,128)(2,1)S(1)}, bf16[160,1176]{1,0:T(8,128)(2,1)}, u32[]{:S(2)}, u32[]{:S(2)}) collective-permute-start(bf16[160,1176]{1,0:T(8,128)(2,1)S(1)} %collective-permute-done.3.refs_2_), channel_id=1, source_target_pairs={{0,16},{16,0},{1,17},{17,1},{2,18},{18,2},{3,19},{19,3},{4,20},{20... | collective-permute-start | bytes 1128968 | tf_op jit(solution)/shard_map/ppermute | solution.py:464
  92.1 4.1 %collective-permute-start.7 = (bf16[512,1280]{1,0:T(8,128)(2,1)S(1)}, bf16[512,1280]{1,0:T(8,128)(2,1)S(1)}, u32[]{:S(2)}, u32[]{:S(2)}) collective-permute-start(bf16[512,1280]{1,0:T(8,128)(2,1)S(1)} %get-tuple-element.26.grad_ref), channel_id=1, source_target_pairs={{0,16},{16,0},{1,17},{17,1},{2,18},{18,2},{3,19},{19,3},{4,20},{20... | collective-permute-start | bytes 3932168 | tf_op jit(solution)/shard_map/ppermute | solution.py:471
  92.2 4.0 %collective-permute-start.8 = (bf16[512,640]{1,0:T(8,128)(2,1)S(1)}, bf16[512,640]{1,0:T(8,128)(2,1)S(1)}, u32[]{:S(2)}, u32[]{:S(2)}) collective-permute-start(bf16[512,640]{1,0:T(8,128)(2,1)S(1)} %get-tuple-element.29), channel_id=1, source_target_pairs={{0,16},{16,0},{1,17},{17,1},{2,18},{18,2},{3,19},{19,3},{4,20},{20... | collective-permute-start | bytes 1966088 | tf_op jit(solution)/shard_map/ppermute | solution.py:470
  98.4 8.4 %collective-permute-start.9 = (bf16[1600,128]{1,0:T(8,128)(2,1)S(1)}, bf16[1600,128]{1,0:T(8,128)(2,1)S(1)}, u32[]{:S(2)}, u32[]{:S(2)}) collective-permute-start(bf16[1600,128]{1,0:T(8,128)(2,1)S(1)} %get-tuple-element.31), channel_id=1, source_target_pairs={{0,1},{16,20},{1,2},{17,21},{2,3},{18,22},{3,0},{19,23},{4,5},{20,... | collective-permute-start | bytes 1228808 | tf_op jit(solution)/shard_map/ppermute | solution.py:473
  99.6 10.8 %collective-permute-start.10 = (bf16[1600,128]{1,0:T(8,128)(2,1)S(1)}, bf16[1600,128]{1,0:T(8,128)(2,1)S(1)}, u32[]{:S(2)}, u32[]{:S(2)}) collective-permute-start(bf16[1600,128]{1,0:T(8,128)(2,1)S(1)} %get-tuple-element.32), channel_id=1, source_target_pairs={{0,3},{16,28},{1,0},{17,29},{2,1},{18,30},{3,2},{19,31},{4,7},{20,... | collective-permute-start | bytes 1228808 | tf_op jit(solution)/shard_map/ppermute | solution.py:473
  101.1 10.7 %collective-permute-start.11 = (bf16[1600,128]{1,0:T(8,128)(2,1)S(1)}, bf16[1600,128]{1,0:T(8,128)(2,1)S(1)}, u32[]{:S(2)}, u32[]{:S(2)}) collective-permute-start(bf16[1600,128]{1,0:T(8,128)(2,1)S(1)} %get-tuple-element.33), channel_id=1, source_target_pairs={{0,2},{16,24},{1,3},{17,25},{2,0},{18,26},{3,1},{19,27},{4,6},{20,... | collective-permute-start | bytes 1228808 | tf_op jit(solution)/shard_map/ppermute | solution.py:473
  112.6 5.1 %collective-permute-start.12 = (bf16[400,128]{1,0:T(8,128)(2,1)S(1)}, bf16[400,128]{1,0:T(8,128)(2,1)S(1)}, u32[]{:S(2)}, u32[]{:S(2)}) collective-permute-start(bf16[400,128]{1,0:T(8,128)(2,1)S(1)} %get-tuple-element.35), channel_id=1, source_target_pairs={{0,4},{16,17},{1,5},{17,18},{2,6},{18,19},{3,7},{19,16},{4,8},{20,... | collective-permute-start | bytes 307208 | tf_op jit(solution)/shard_map/ppermute | solution.py:475
  112.7 5.4 %collective-permute-start.13 = (bf16[400,128]{1,0:T(8,128)(2,1)S(1)}, bf16[400,128]{1,0:T(8,128)(2,1)S(1)}, u32[]{:S(2)}, u32[]{:S(2)}) collective-permute-start(bf16[400,128]{1,0:T(8,128)(2,1)S(1)} %get-tuple-element.36), channel_id=1, source_target_pairs={{0,12},{16,19},{1,13},{17,16},{2,14},{18,17},{3,15},{19,18},{4,0},... | collective-permute-start | bytes 307208 | tf_op jit(solution)/shard_map/ppermute | solution.py:475
  115.4 5.0 %collective-permute-start.14 = (bf16[400,128]{1,0:T(8,128)(2,1)S(1)}, bf16[400,128]{1,0:T(8,128)(2,1)S(1)}, u32[]{:S(2)}, u32[]{:S(2)}) collective-permute-start(bf16[400,128]{1,0:T(8,128)(2,1)S(1)} %get-tuple-element.37), channel_id=1, source_target_pairs={{0,8},{16,18},{1,9},{17,19},{2,10},{18,16},{3,11},{19,17},{4,12},{... | collective-permute-start | bytes 307208 | tf_op jit(solution)/shard_map/ppermute | solution.py:475
  143.8 8.1 %collective-permute-start.17 = (f32[400,128]{1,0:T(8,128)S(1)}, f32[400,128]{1,0:T(8,128)S(1)}, u32[]{:S(2)}, u32[]{:S(2)}) collective-permute-start(f32[400,128]{1,0:T(8,128)S(1)} %slice.8.refs_0_), channel_id=1, source_target_pairs={{0,12},{4,0},{8,4},{12,8},{1,13},{5,1},{9,5},{13,9},{2,14},{6,2},{... | collective-permute-start | bytes 614408 | tf_op jit(solution)/shard_map/ppermute | solution.py:480
  146.6 9.7 %collective-permute-start.16 = (f32[400,128]{1,0:T(8,128)S(1)}, f32[400,128]{1,0:T(8,128)S(1)}, u32[]{:S(2)}, u32[]{:S(2)}) collective-permute-start(f32[400,128]{1,0:T(8,128)S(1)} %slice.8.refs_0_), channel_id=1, source_target_pairs={{0,8},{4,12},{8,0},{12,4},{1,9},{5,13},{9,1},{13,5},{2,10},{6,14},... | collective-permute-start | bytes 614408 | tf_op jit(solution)/shard_map/ppermute | solution.py:480
  147.3 10.8 %collective-permute-start.15 = (f32[400,128]{1,0:T(8,128)S(1)}, f32[400,128]{1,0:T(8,128)S(1)}, u32[]{:S(2)}, u32[]{:S(2)}) collective-permute-start(f32[400,128]{1,0:T(8,128)S(1)} %slice.8.refs_0_), channel_id=1, source_target_pairs={{0,4},{4,8},{8,12},{12,0},{1,5},{5,9},{9,13},{13,1},{2,6},{6,10},{... | collective-permute-start | bytes 614408 | tf_op jit(solution)/shard_map/ppermute | solution.py:480
  147.3 12.9 %collective-permute-start.18 = (f32[400,128]{1,0:T(8,128)S(1)}, f32[400,128]{1,0:T(8,128)S(1)}, u32[]{:S(2)}, u32[]{:S(2)}) collective-permute-start(f32[400,128]{1,0:T(8,128)S(1)} %slice.8.refs_0_), channel_id=1, source_target_pairs={{0,16},{16,0},{1,17},{17,1},{2,18},{18,2},{3,19},{19,3},{4,20},{20... | collective-permute-start | bytes 614408 | tf_op jit(solution)/shard_map/ppermute | solution.py:481
  151.9 8.3 %collective-permute-start.21 = (f32[400,128]{1,0:T(8,128)S(1)}, f32[400,128]{1,0:T(8,128)S(1)}, u32[]{:S(2)}, u32[]{:S(2)}) collective-permute-start(f32[400,128]{1,0:T(8,128)S(1)} %collective-permute-done.17.refs_3_), channel_id=1, source_target_pairs={{0,16},{16,0},{1,17},{17,1},{2,18},{18,2},{3,19},{19,3},{4,20},{20... | collective-permute-start | bytes 614408 | tf_op jit(solution)/shard_map/ppermute | solution.py:481
  156.3 3.9 %collective-permute-start.20 = (f32[400,128]{1,0:T(8,128)S(1)}, f32[400,128]{1,0:T(8,128)S(1)}, u32[]{:S(2)}, u32[]{:S(2)}) collective-permute-start(f32[400,128]{1,0:T(8,128)S(1)} %collective-permute-done.16.refs_2_), channel_id=1, source_target_pairs={{0,16},{16,0},{1,17},{17,1},{2,18},{18,2},{3,19},{19,3},{4,20},{20... | collective-permute-start | bytes 614408 | tf_op jit(solution)/shard_map/ppermute | solution.py:481
  158.1 3.2 %collective-permute-start.19 = (f32[400,128]{1,0:T(8,128)S(1)}, f32[400,128]{1,0:T(8,128)S(1)}, u32[]{:S(2)}, u32[]{:S(2)}) collective-permute-start(f32[400,128]{1,0:T(8,128)S(1)} %collective-permute-done.15.refs_1_), channel_id=1, source_target_pairs={{0,16},{16,0},{1,17},{17,1},{2,18},{18,2},{3,19},{19,3},{4,20},{20... | collective-permute-start | bytes 614408 | tf_op jit(solution)/shard_map/ppermute | solution.py:481
  (10 other events, 122.6 us)

commit v3 on v2

--- a/solution.py
+++ b/solution.py
@@ -28,7 +28,7 @@
 QUARTER = LINE // 4
 STEP = 80
 PIECE = 56
-BLOCK = 256
+BLOCK = 512
 SUMS = 96
 ALL = pl.BlockSpec(memory_space=pltpu.VMEM)
 FAR = pl.BlockSpec(memory_space=pltpu.HBM)

time: 164 us -> 164 us (level)
  no operation moved by 1% of the time
where the time goes in v3:
time: 164 us
  waiting for transfers between devices  48.8 us (30%)
  starting transfers between devices  46.2 us (28%)
  Pallas kernels  42 us (26%)
  blocking collectives  23.3 us (14%)
  local copies, waits for them, and re-layouts  2.64 us (2%)
    ppermute x4, starting transfers between devices, shards(): lax.ppermute(part, 'core', swap)  12.9 us
    all_to_all x1, blocking collectives, shards(): lax.all_to_all(quarter.reshape(8, PIECE, 128), 'z', 0, 0, tiled=True)  11.9 us
    all_to_all x1, blocking collectives, copies(): return lax.all_to_all(array, axis, 0, 0, tiled=True)  11.4 us
    all_to_all x1, waiting for transfers between devices, shards(): arrived1 = lax.all_to_all(packed1, ('z', 'core'), 0, 0, tiled=True)  11.1 us
    pallas_call x2, Pallas kernels, packed_rows(): pl.pallas_call(patch_kernel, out_shape=jax.ShapeDtypeStruct(shape, jnp.bf...  10.8 us
    all_to_all x1, starting transfers between devices, shards(): arrived0 = lax.all_to_all(packed0, ('z', 'core'), 0, 0, tiled=True)  10.1 us
    ppermute x3, waiting for transfers between devices, shards(): parts = [lax.ppermute(part, 'fsdp', ring(by)) for by in (1, 2, 3)]  9.68 us
    ppermute x3, waiting for transfers between devices, shards(): lax.ppermute(sent[by - 1], plane, plane_shift(by, 0))  9.18 us
  transfers between devices with their start and end apart: 24, of which 15 were waited for; matrix products, arithmetic and copies ran while one was open for 2% of the time, Pallas kernels for 15%

profile of v3, /device:TPU:1, one launch (start us, length us, event | category | flops | bytes accessed | tf_op | source)
XLA Modules:
  0.0 163.8 jit_solution(5548422407540131674)
XLA Ops:
  0.6 5.3 %patch_rows.2 = bf16[16,296,128]{2,1,0:T(8,128)(2,1)} custom-call(s32[1]{0:T(128)} %constant.22.clone.1.valid_ref, s32[1,512]{1,0:T(1,128)} %bitcast.12, bf16[1,1,4,3,224,224]{5,4,3,2,1,0:T(8,128)(2,1)} %fb_ref.3, bf16[1,1,4,3,224,224]{5,4,3,2,1,0:T(8,128)(2,1)} %fb_ref.3), custom_call_target="tpu_custom_call" | custom-call | tf_op jit(solution)/shard_map/patch_rows/pallas_call | solution.py:119
  6.0 10.1 %all-to-all-start.1 = ((bf16[16,296,128]{2,1,0:T(8,128)(2,1)}), bf16[16,296,128]{2,1,0:T(8,128)(2,1)S(1)}, u32[]{:S(2)}, u32[]{:S(2)}) async-start(bf16[16,296,128]{2,1,0:T(8,128)(2,1)} %patch_rows.2), calls=%async_computation.1 | async-start | bytes 2424832 | tf_op jit(solution)/shard_map/all_to_all | solution.py:457
  16.1 2.8 %collective-permute-start.3 = (bf16[160,1176]{1,0:T(8,128)(2,1)S(1)}, bf16[160,1176]{1,0:T(8,128)(2,1)S(1)}, u32[]{:S(2)}, u32[]{:S(2)}) collective-permute-start(bf16[160,1176]{1,0:T(8,128)(2,1)S(1)} %constant_dynamic-slice_fusion), channel_id=1, source_target_pairs={{0,3},{1,0},{2,1},{3,2},{4,7},{5,4},{6,5},{7,6},{8,11},{9,8},{10,9... | collective-permute-start | bytes 1128968 | tf_op jit(solution)/shard_map/ppermute | solution.py:460
  22.3 8.7 %collective-permute-done.fa_ref = bf16[1,1,1,3,224,224]{5,4,3,2,1,0:T(8,128)(2,1)S(1)} collective-permute-done((bf16[1,1,1,3,224,224]{5,4,3,2,1,0:T(8,128)(2,1)S(1)}, bf16[1,1,1,3,224,224]{5,4,3,2,1,0:T(8,128)(2,1)S(1)}, u32[]{:S(2)}, u32[]{:S(2)}) %collective-permute-start) | collective-permute-done | bytes 301088 | tf_op jit(solution)/shard_map/ppermute | solution.py:452
  31.0 5.5 %collective-permute-done.3.refs_2_ = bf16[160,1176]{1,0:T(8,128)(2,1)S(1)} collective-permute-done((bf16[160,1176]{1,0:T(8,128)(2,1)S(1)}, bf16[160,1176]{1,0:T(8,128)(2,1)S(1)}, u32[]{:S(2)}, u32[]{:S(2)}) %collective-permute-start.3) | collective-permute-done | bytes 376352 | tf_op jit(solution)/shard_map/ppermute | solution.py:460
  36.4 4.2 %collective-permute-done.1.refs_0_ = bf16[160,1176]{1,0:T(8,128)(2,1)S(1)} collective-permute-done((bf16[160,1176]{1,0:T(8,128)(2,1)S(1)}, bf16[160,1176]{1,0:T(8,128)(2,1)S(1)}, u32[]{:S(2)}, u32[]{:S(2)}) %collective-permute-start.1) | collective-permute-done | bytes 376352 | tf_op jit(solution)/shard_map/ppermute | solution.py:460
  40.7 5.5 %patch_rows.3 = bf16[16,296,128]{2,1,0:T(8,128)(2,1)} custom-call(s32[1]{0:T(128)} %bitcast.6.valid_ref, s32[1,512]{1,0:T(1,128)} %bitcast.13, bf16[1,1,1,3,224,224]{5,4,3,2,1,0:T(8,128)(2,1)} %copy-done.7, bf16[1,1,4,3,224,224]{5,4,3,2,1,0:T(8,128)(2,1)} %fb_ref.3), custom_call_target="tpu_custom_call" | custom-call | tf_op jit(solution)/shard_map/patch_rows/pallas_call | solution.py:119
  47.3 6.2 %all-to-all-start = ((bf16[16,296,128]{2,1,0:T(8,128)(2,1)}), bf16[16,296,128]{2,1,0:T(8,128)(2,1)S(1)}, u32[]{:S(2)}, u32[]{:S(2)}) async-start(bf16[16,296,128]{2,1,0:T(8,128)(2,1)} %patch_rows.3), calls=%async_computation | async-start | bytes 2424832 | tf_op jit(solution)/shard_map/all_to_all | solution.py:463
  56.6 9.1 %weight_columns.1.w_ref.w_far = bf16[1280,1280]{1,0:T(8,128)(2,1)} custom-call(s32[5]{0:T(128)} %stack.23.place_ref.core_ref, s32[1,1176]{1,0:T(1,128)} %constant.26.clone.column_ref, bf16[320,1176]{1,0:T(8,128)(2,1)} %own_ref.1, bf16[160,1176]{1,0:T(8,128)(2,1)} %copy-done.6, bf16[160,1176]{1,0:T(8,128)(2,1)} %copy-done.5, bf16[160,1176]{1,0:T(8,128)(2,1)} %copy-done.4, ...), custom_call_target="tpu_custom_call" | custom-call | tf_op jit(solution)/shard_map/weight_columns/pallas_call | solution.py:154
  65.6 8.0 %first_half.1.part_far = f32[512,1920]{1,0:T(8,128)} custom-call(s32[512,1]{1,0:T(8,128)} %copy.11.slot_ref, bf16[16,296,128]{2,1,0:T(8,128)(2,1)} %copy-done.2, bf16[1280,1280]{1,0:T(8,128)(2,1)} %weight_columns.1.w_ref.w_far), custom_call_target="tpu_custom_call" | custom-call | tf_op jit(solution)/shard_map/first_half/pallas_call | solution.py:192
  73.7 11.1 %all-to-all-done.arr_ref = bf16[16,296,128]{2,1,0:T(8,128)(2,1)S(1)} async-done(((bf16[16,296,128]{2,1,0:T(8,128)(2,1)}), bf16[16,296,128]{2,1,0:T(8,128)(2,1)S(1)}, u32[]{:S(2)}, u32[]{:S(2)}) %all-to-all-start) | async-done | bytes 1212448 | tf_op jit(solution)/shard_map/all_to_all | solution.py:463
  84.7 7.1 %norm_backward.1 = (bf16[512,1280]{1,0:T(8,128)(2,1)S(1)}, bf16[512,640]{1,0:T(8,128)(2,1)S(1)}, bf16[512,640]{1,0:T(8,128)(2,1)S(1)}, f32[16,1280]{1,0:T(8,128)S(1)}) custom-call(s32[5]{0:T(128)S(1)} %copy-done.1, s32[512,1]{1,0:T(8,128)S(1)} %copy-done, bf16[16,296,128]{2,1,0:T(8,128)(2,1)S(1)} %all-to-all-done.arr_ref, f32[512,1920]{1,0:T(8,128)} %first_half.1.part_far, ...), custom_call_target="tpu_custom_call" | custom-call | tf_op jit(solution)/shard_map/norm_backward/pallas_call | solution.py:258
  93.7 2.2 %collective-permute-done.8.rows_ref = bf16[512,640]{1,0:T(8,128)(2,1)S(1)} collective-permute-done((bf16[512,640]{1,0:T(8,128)(2,1)S(1)}, bf16[512,640]{1,0:T(8,128)(2,1)S(1)}, u32[]{:S(2)}, u32[]{:S(2)}) %collective-permute-start.8) | collective-permute-done | bytes 655392 | tf_op jit(solution)/shard_map/ppermute | solution.py:470
  102.4 4.1 %collective-permute-done.9.in1_ref = bf16[1600,128]{1,0:T(8,128)(2,1)S(1)} collective-permute-done((bf16[1600,128]{1,0:T(8,128)(2,1)S(1)}, bf16[1600,128]{1,0:T(8,128)(2,1)S(1)}, u32[]{:S(2)}, u32[]{:S(2)}) %collective-permute-start.9) | collective-permute-done | bytes 409632 | tf_op jit(solution)/shard_map/ppermute | solution.py:473
  106.5 3.7 %collective-permute-done.10.in2_ref = bf16[1600,128]{1,0:T(8,128)(2,1)S(1)} collective-permute-done((bf16[1600,128]{1,0:T(8,128)(2,1)S(1)}, bf16[1600,128]{1,0:T(8,128)(2,1)S(1)}, u32[]{:S(2)}, u32[]{:S(2)}) %collective-permute-start.10) | collective-permute-done | bytes 409632 | tf_op jit(solution)/shard_map/ppermute | solution.py:473
  112.4 2.7 %collective-permute-start.13 = (bf16[400,128]{1,0:T(8,128)(2,1)S(1)}, bf16[400,128]{1,0:T(8,128)(2,1)S(1)}, u32[]{:S(2)}, u32[]{:S(2)}) collective-permute-start(bf16[400,128]{1,0:T(8,128)(2,1)S(1)} %get-tuple-element.36), channel_id=1, source_target_pairs={{0,12},{16,19},{1,13},{17,16},{2,14},{18,17},{3,15},{19,18},{4,0},... | collective-permute-start | bytes 307208 | tf_op jit(solution)/shard_map/ppermute | solution.py:475
  115.1 2.3 %collective-permute-done.12 = bf16[400,128]{1,0:T(8,128)(2,1)S(1)} collective-permute-done((bf16[400,128]{1,0:T(8,128)(2,1)S(1)}, bf16[400,128]{1,0:T(8,128)(2,1)S(1)}, u32[]{:S(2)}, u32[]{:S(2)}) %collective-permute-start.12) | collective-permute-done | bytes 102432 | tf_op jit(solution)/shard_map/ppermute | solution.py:475
  117.8 2.3 %collective-permute-done.14 = bf16[400,128]{1,0:T(8,128)(2,1)S(1)} collective-permute-done((bf16[400,128]{1,0:T(8,128)(2,1)S(1)}, bf16[400,128]{1,0:T(8,128)(2,1)S(1)}, u32[]{:S(2)}, u32[]{:S(2)}) %collective-permute-start.14) | collective-permute-done | bytes 102432 | tf_op jit(solution)/shard_map/ppermute | solution.py:475
  120.2 11.9 %all_to_all.20 = f32[8,56,128]{2,1,0:T(8,128)S(1)} all-to-all(f32[8,56,128]{2,1,0:T(8,128)S(1)} %bitcast.10), channel_id=1, replica_groups=mesh['z'=8,'core'=2,'slab'=4,'fsdp'=4] {'z'}, dimensions={0} | all-to-all | bytes 458752 | tf_op jit(solution)/shard_map/all_to_all | solution.py:478
  132.1 11.4 %all_to_all.21 = f32[8,56,128]{2,1,0:T(8,128)S(1)} all-to-all(f32[8,56,128]{2,1,0:T(8,128)S(1)} %broadcast_in_dim.13), channel_id=1, replica_groups=mesh['z'=8,'core'=2,'slab'=4,'fsdp'=4] {'z'}, dimensions={0} | all-to-all | bytes 458752 | tf_op jit(solution)/shard_map/all_to_all | solution.py:443
  143.6 2.8 %collective-permute-start.17 = (f32[400,128]{1,0:T(8,128)S(1)}, f32[400,128]{1,0:T(8,128)S(1)}, u32[]{:S(2)}, u32[]{:S(2)}) collective-permute-start(f32[400,128]{1,0:T(8,128)S(1)} %slice.8.refs_0_), channel_id=1, source_target_pairs={{0,12},{4,0},{8,4},{12,8},{1,13},{5,1},{9,5},{13,9},{2,14},{6,2},{... | collective-permute-start | bytes 614408 | tf_op jit(solution)/shard_map/ppermute | solution.py:480
  147.1 4.6 %collective-permute-start.18 = (f32[400,128]{1,0:T(8,128)S(1)}, f32[400,128]{1,0:T(8,128)S(1)}, u32[]{:S(2)}, u32[]{:S(2)}) collective-permute-start(f32[400,128]{1,0:T(8,128)S(1)} %slice.8.refs_0_), channel_id=1, source_target_pairs={{0,16},{16,0},{1,17},{17,1},{2,18},{18,2},{3,19},{19,3},{4,20},{20... | collective-permute-start | bytes 614408 | tf_op jit(solution)/shard_map/ppermute | solution.py:481
  151.6 4.4 %collective-permute-start.21 = (f32[400,128]{1,0:T(8,128)S(1)}, f32[400,128]{1,0:T(8,128)S(1)}, u32[]{:S(2)}, u32[]{:S(2)}) collective-permute-start(f32[400,128]{1,0:T(8,128)S(1)} %collective-permute-done.17.refs_3_), channel_id=1, source_target_pairs={{0,16},{16,0},{1,17},{17,1},{2,18},{18,2},{3,19},{19,3},{4,20},{20... | collective-permute-start | bytes 614408 | tf_op jit(solution)/shard_map/ppermute | solution.py:481
  161.0 2.7 %column_order.1 = (f32[320,1176]{1,0:T(8,128)}, f32[2,320]{1,0:T(2,128)}) custom-call(s32[5]{0:T(128)S(1)} %copy-done.1, f32[400,128]{1,0:T(8,128)S(1)} %slice.8.refs_0_, f32[400,128]{1,0:T(8,128)S(1)} %collective-permute-done.15.refs_1_, f32[400,128]{1,0:T(8,128)S(1)} %collective-permute-done.16.refs_2_, f32[400,128]{1,0:T(8,128)S(1)} %collective-permute-done.17.refs_3_, ...), custom_call_target="tpu_custom_call" | custom-call | tf_op jit(solution)/shard_map/column_order/pallas_call | solution.py:406
  (65 shorter events, 24.2 us)
Async XLA Ops:
  6.0 41.3 %all-to-all-start.1 = ((bf16[16,296,128]{2,1,0:T(8,128)(2,1)}), bf16[16,296,128]{2,1,0:T(8,128)(2,1)S(1)}, u32[]{:S(2)}, u32[]{:S(2)}) async-start(bf16[16,296,128]{2,1,0:T(8,128)(2,1)} %patch_rows.2), calls=%async_computation.1 | async-start | bytes 2424832 | tf_op jit(solution)/shard_map/all_to_all | solution.py:457
  16.1 20.3 %collective-permute-start.3 = (bf16[160,1176]{1,0:T(8,128)(2,1)S(1)}, bf16[160,1176]{1,0:T(8,128)(2,1)S(1)}, u32[]{:S(2)}, u32[]{:S(2)}) collective-permute-start(bf16[160,1176]{1,0:T(8,128)(2,1)S(1)} %constant_dynamic-slice_fusion), channel_id=1, source_target_pairs={{0,3},{1,0},{2,1},{3,2},{4,7},{5,4},{6,5},{7,6},{8,11},{9,8},{10,9... | collective-permute-start | bytes 1128968 | tf_op jit(solution)/shard_map/ppermute | solution.py:460
  19.0 17.4 %collective-permute-start.2 = (bf16[160,1176]{1,0:T(8,128)(2,1)S(1)}, bf16[160,1176]{1,0:T(8,128)(2,1)S(1)}, u32[]{:S(2)}, u32[]{:S(2)}) collective-permute-start(bf16[160,1176]{1,0:T(8,128)(2,1)S(1)} %constant_dynamic-slice_fusion), channel_id=1, source_target_pairs={{0,2},{1,3},{2,0},{3,1},{4,6},{5,7},{6,4},{7,5},{8,10},{9,11},{10,... | collective-permute-start | bytes 1128968 | tf_op jit(solution)/shard_map/ppermute | solution.py:460
  19.3 21.3 %collective-permute-start.1 = (bf16[160,1176]{1,0:T(8,128)(2,1)S(1)}, bf16[160,1176]{1,0:T(8,128)(2,1)S(1)}, u32[]{:S(2)}, u32[]{:S(2)}) collective-permute-start(bf16[160,1176]{1,0:T(8,128)(2,1)S(1)} %constant_dynamic-slice_fusion), channel_id=1, source_target_pairs={{0,1},{1,2},{2,3},{3,0},{4,5},{5,6},{6,7},{7,4},{8,9},{9,10},{10,1... | collective-permute-start | bytes 1128968 | tf_op jit(solution)/shard_map/ppermute | solution.py:460
  21.0 9.9 %collective-permute-start = (bf16[1,1,1,3,224,224]{5,4,3,2,1,0:T(8,128)(2,1)S(1)}, bf16[1,1,1,3,224,224]{5,4,3,2,1,0:T(8,128)(2,1)S(1)}, u32[]{:S(2)}, u32[]{:S(2)}) collective-permute-start(bf16[1,1,1,3,224,224]{5,4,3,2,1,0:T(8,128)(2,1)S(1)} %slice.6), channel_id=1, source_target_pairs={{0,4},{4,8},{8,12},{12,0},{1,5},{5,9},{9,13},{13,1},{2,6},{6,10},{... | collective-permute-start | bytes 903176 | tf_op jit(solution)/shard_map/ppermute | solution.py:452
  47.3 37.4 %all-to-all-start = ((bf16[16,296,128]{2,1,0:T(8,128)(2,1)}), bf16[16,296,128]{2,1,0:T(8,128)(2,1)S(1)}, u32[]{:S(2)}, u32[]{:S(2)}) async-start(bf16[16,296,128]{2,1,0:T(8,128)(2,1)} %patch_rows.3), calls=%async_computation | async-start | bytes 2424832 | tf_op jit(solution)/shard_map/all_to_all | solution.py:463
  53.5 2.3 %collective-permute-start.4 = (bf16[160,1176]{1,0:T(8,128)(2,1)}, bf16[160,1176]{1,0:T(8,128)(2,1)}, u32[]{:S(2)}, u32[]{:S(2)}) collective-permute-start(bf16[160,1176]{1,0:T(8,128)(2,1)} %copy-done.6), channel_id=1, source_target_pairs={{0,16},{16,0},{1,17},{17,1},{2,18},{18,2},{3,19},{19,3},{4,20},{20... | collective-permute-start | bytes 1128968 | tf_op jit(solution)/shard_map/ppermute | solution.py:464
  53.7 2.3 %collective-permute-start.5 = (bf16[160,1176]{1,0:T(8,128)(2,1)S(1)}, bf16[160,1176]{1,0:T(8,128)(2,1)}, u32[]{:S(2)}, u32[]{:S(2)}) collective-permute-start(bf16[160,1176]{1,0:T(8,128)(2,1)S(1)} %collective-permute-done.2.refs_1_), channel_id=1, source_target_pairs={{0,16},{16,0},{1,17},{17,1},{2,18},{18,2},{3,19},{19,3},{4,20},{20... | collective-permute-start | bytes 1128968 | tf_op jit(solution)/shard_map/ppermute | solution.py:464
  54.0 2.5 %collective-permute-start.6 = (bf16[160,1176]{1,0:T(8,128)(2,1)S(1)}, bf16[160,1176]{1,0:T(8,128)(2,1)}, u32[]{:S(2)}, u32[]{:S(2)}) collective-permute-start(bf16[160,1176]{1,0:T(8,128)(2,1)S(1)} %collective-permute-done.3.refs_2_), channel_id=1, source_target_pairs={{0,16},{16,0},{1,17},{17,1},{2,18},{18,2},{3,19},{19,3},{4,20},{20... | collective-permute-start | bytes 1128968 | tf_op jit(solution)/shard_map/ppermute | solution.py:464
  91.9 4.1 %collective-permute-start.7 = (bf16[512,1280]{1,0:T(8,128)(2,1)S(1)}, bf16[512,1280]{1,0:T(8,128)(2,1)S(1)}, u32[]{:S(2)}, u32[]{:S(2)}) collective-permute-start(bf16[512,1280]{1,0:T(8,128)(2,1)S(1)} %get-tuple-element.26.grad_ref), channel_id=1, source_target_pairs={{0,16},{16,0},{1,17},{17,1},{2,18},{18,2},{3,19},{19,3},{4,20},{20... | collective-permute-start | bytes 3932168 | tf_op jit(solution)/shard_map/ppermute | solution.py:471
  92.0 4.0 %collective-permute-start.8 = (bf16[512,640]{1,0:T(8,128)(2,1)S(1)}, bf16[512,640]{1,0:T(8,128)(2,1)S(1)}, u32[]{:S(2)}, u32[]{:S(2)}) collective-permute-start(bf16[512,640]{1,0:T(8,128)(2,1)S(1)} %get-tuple-element.29), channel_id=1, source_target_pairs={{0,16},{16,0},{1,17},{17,1},{2,18},{18,2},{3,19},{19,3},{4,20},{20... | collective-permute-start | bytes 1966088 | tf_op jit(solution)/shard_map/ppermute | solution.py:470
  98.1 8.4 %collective-permute-start.9 = (bf16[1600,128]{1,0:T(8,128)(2,1)S(1)}, bf16[1600,128]{1,0:T(8,128)(2,1)S(1)}, u32[]{:S(2)}, u32[]{:S(2)}) collective-permute-start(bf16[1600,128]{1,0:T(8,128)(2,1)S(1)} %get-tuple-element.31), channel_id=1, source_target_pairs={{0,1},{16,20},{1,2},{17,21},{2,3},{18,22},{3,0},{19,23},{4,5},{20,... | collective-permute-start | bytes 1228808 | tf_op jit(solution)/shard_map/ppermute | solution.py:473
  99.4 10.8 %collective-permute-start.10 = (bf16[1600,128]{1,0:T(8,128)(2,1)S(1)}, bf16[1600,128]{1,0:T(8,128)(2,1)S(1)}, u32[]{:S(2)}, u32[]{:S(2)}) collective-permute-start(bf16[1600,128]{1,0:T(8,128)(2,1)S(1)} %get-tuple-element.32), channel_id=1, source_target_pairs={{0,3},{16,28},{1,0},{17,29},{2,1},{18,30},{3,2},{19,31},{4,7},{20,... | collective-permute-start | bytes 1228808 | tf_op jit(solution)/shard_map/ppermute | solution.py:473
  100.9 10.7 %collective-permute-start.11 = (bf16[1600,128]{1,0:T(8,128)(2,1)S(1)}, bf16[1600,128]{1,0:T(8,128)(2,1)S(1)}, u32[]{:S(2)}, u32[]{:S(2)}) collective-permute-start(bf16[1600,128]{1,0:T(8,128)(2,1)S(1)} %get-tuple-element.33), channel_id=1, source_target_pairs={{0,2},{16,24},{1,3},{17,25},{2,0},{18,26},{3,1},{19,27},{4,6},{20,... | collective-permute-start | bytes 1228808 | tf_op jit(solution)/shard_map/ppermute | solution.py:473
  112.3 5.1 %collective-permute-start.12 = (bf16[400,128]{1,0:T(8,128)(2,1)S(1)}, bf16[400,128]{1,0:T(8,128)(2,1)S(1)}, u32[]{:S(2)}, u32[]{:S(2)}) collective-permute-start(bf16[400,128]{1,0:T(8,128)(2,1)S(1)} %get-tuple-element.35), channel_id=1, source_target_pairs={{0,4},{16,17},{1,5},{17,18},{2,6},{18,19},{3,7},{19,16},{4,8},{20,... | collective-permute-start | bytes 307208 | tf_op jit(solution)/shard_map/ppermute | solution.py:475
  112.4 5.4 %collective-permute-start.13 = (bf16[400,128]{1,0:T(8,128)(2,1)S(1)}, bf16[400,128]{1,0:T(8,128)(2,1)S(1)}, u32[]{:S(2)}, u32[]{:S(2)}) collective-permute-start(bf16[400,128]{1,0:T(8,128)(2,1)S(1)} %get-tuple-element.36), channel_id=1, source_target_pairs={{0,12},{16,19},{1,13},{17,16},{2,14},{18,17},{3,15},{19,18},{4,0},... | collective-permute-start | bytes 307208 | tf_op jit(solution)/shard_map/ppermute | solution.py:475
  115.1 5.0 %collective-permute-start.14 = (bf16[400,128]{1,0:T(8,128)(2,1)S(1)}, bf16[400,128]{1,0:T(8,128)(2,1)S(1)}, u32[]{:S(2)}, u32[]{:S(2)}) collective-permute-start(bf16[400,128]{1,0:T(8,128)(2,1)S(1)} %get-tuple-element.37), channel_id=1, source_target_pairs={{0,8},{16,18},{1,9},{17,19},{2,10},{18,16},{3,11},{19,17},{4,12},{... | collective-permute-start | bytes 307208 | tf_op jit(solution)/shard_map/ppermute | solution.py:475
  143.6 8.1 %collective-permute-start.17 = (f32[400,128]{1,0:T(8,128)S(1)}, f32[400,128]{1,0:T(8,128)S(1)}, u32[]{:S(2)}, u32[]{:S(2)}) collective-permute-start(f32[400,128]{1,0:T(8,128)S(1)} %slice.8.refs_0_), channel_id=1, source_target_pairs={{0,12},{4,0},{8,4},{12,8},{1,13},{5,1},{9,5},{13,9},{2,14},{6,2},{... | collective-permute-start | bytes 614408 | tf_op jit(solution)/shard_map/ppermute | solution.py:480
  146.4 9.7 %collective-permute-start.16 = (f32[400,128]{1,0:T(8,128)S(1)}, f32[400,128]{1,0:T(8,128)S(1)}, u32[]{:S(2)}, u32[]{:S(2)}) collective-permute-start(f32[400,128]{1,0:T(8,128)S(1)} %slice.8.refs_0_), channel_id=1, source_target_pairs={{0,8},{4,12},{8,0},{12,4},{1,9},{5,13},{9,1},{13,5},{2,10},{6,14},... | collective-permute-start | bytes 614408 | tf_op jit(solution)/shard_map/ppermute | solution.py:480
  147.1 10.8 %collective-permute-start.15 = (f32[400,128]{1,0:T(8,128)S(1)}, f32[400,128]{1,0:T(8,128)S(1)}, u32[]{:S(2)}, u32[]{:S(2)}) collective-permute-start(f32[400,128]{1,0:T(8,128)S(1)} %slice.8.refs_0_), channel_id=1, source_target_pairs={{0,4},{4,8},{8,12},{12,0},{1,5},{5,9},{9,13},{13,1},{2,6},{6,10},{... | collective-permute-start | bytes 614408 | tf_op jit(solution)/shard_map/ppermute | solution.py:480
  147.1 12.9 %collective-permute-start.18 = (f32[400,128]{1,0:T(8,128)S(1)}, f32[400,128]{1,0:T(8,128)S(1)}, u32[]{:S(2)}, u32[]{:S(2)}) collective-permute-start(f32[400,128]{1,0:T(8,128)S(1)} %slice.8.refs_0_), channel_id=1, source_target_pairs={{0,16},{16,0},{1,17},{17,1},{2,18},{18,2},{3,19},{19,3},{4,20},{20... | collective-permute-start | bytes 614408 | tf_op jit(solution)/shard_map/ppermute | solution.py:481
  151.6 8.3 %collective-permute-start.21 = (f32[400,128]{1,0:T(8,128)S(1)}, f32[400,128]{1,0:T(8,128)S(1)}, u32[]{:S(2)}, u32[]{:S(2)}) collective-permute-start(f32[400,128]{1,0:T(8,128)S(1)} %collective-permute-done.17.refs_3_), channel_id=1, source_target_pairs={{0,16},{16,0},{1,17},{17,1},{2,18},{18,2},{3,19},{19,3},{4,20},{20... | collective-permute-start | bytes 614408 | tf_op jit(solution)/shard_map/ppermute | solution.py:481
  156.1 3.9 %collective-permute-start.20 = (f32[400,128]{1,0:T(8,128)S(1)}, f32[400,128]{1,0:T(8,128)S(1)}, u32[]{:S(2)}, u32[]{:S(2)}) collective-permute-start(f32[400,128]{1,0:T(8,128)S(1)} %collective-permute-done.16.refs_2_), channel_id=1, source_target_pairs={{0,16},{16,0},{1,17},{17,1},{2,18},{18,2},{3,19},{19,3},{4,20},{20... | collective-permute-start | bytes 614408 | tf_op jit(solution)/shard_map/ppermute | solution.py:481
  157.9 3.2 %collective-permute-start.19 = (f32[400,128]{1,0:T(8,128)S(1)}, f32[400,128]{1,0:T(8,128)S(1)}, u32[]{:S(2)}, u32[]{:S(2)}) collective-permute-start(f32[400,128]{1,0:T(8,128)S(1)} %collective-permute-done.15.refs_1_), channel_id=1, source_target_pairs={{0,16},{16,0},{1,17},{17,1},{2,18},{18,2},{3,19},{19,3},{4,20},{20... | collective-permute-start | bytes 614408 | tf_op jit(solution)/shard_map/ppermute | solution.py:481
  (10 other events, 122.6 us)
